TPU v7x, 512 devices: a whole 4x8x8 slice. The times are simulated.
512 devices in a mesh: grp: 8 (over z_lo, core), box: 64 (over z_hi, x, y).
Axes of the slice: x: 4, y: 8, z: 8 (z_hi: 2, z_lo: 4; z = z_hi * 4 + z_lo), core: 2. Of those that a mesh axis runs over, the one named last changes fastest.
Arguments:
- coarse_dens: float32 [728, 512], P(None, ('grp', 'box')), may hold values from -6 to 6
- owner_slot: int32 [512], replicated, may hold values from 0 to 511, as said below
- check_to_equiv: float32 [728, 728], replicated, may hold values from -0.21875 to 0.21875
- parent_own: float32 [728, 4096], P(None, ('grp', 'box')), may hold values from -6 to 6
- leaf_own: float32 [728, 32768], P(None, ('grp', 'box')), may hold values from -6 to 6
- leaf_counts: int32 [512, 64], P(('grp', 'box')), may hold values from 1 to 128, 2048 in all within a row
- particles: float32 [3, 1048576], P(None, ('grp', 'box')), may hold values from -0.9 to 0.9
- panels: float32 [4, 524288], P(None, ('grp', 'box')), as said below
- near_part: int32 [32768], P(('grp', 'box')), may hold values from 0 to 15
- near_pan: int32 [32768], P(('grp', 'box')), may hold values from 0 to 23
- near_count: int32 [512], P(('grp', 'box')), may hold values from 8 to 64, as said below
Outputs:
- field_grad: float32 [4, 1048576], P(None, ('grp', 'box'))
Inputs may be any that keep to these rules, and one draw needn't show every extreme that they name: `owner_slot`: a permutation that keeps coarse box k among the 64 slots of group k // 64. `near_count`: some device has all 64 slots live. `panels`: rows 0 to 2 hold a panel centre within 1 in each coordinate of the centre of some leaf of the device that holds the panel; row 3 holds its strength.
All inputs are finite; a program needn't handle non-finite values.
Results may differ from a plain program's by a relative error of at most 0.0003.
Values sent between devices are 32-bit elements; how exact they have to be, the bound alone decides.
A program may use at most 64 MiB of HBM per device.

v0:
```python
import math

import jax
import jax.numpy as jnp
import numpy as np
from jax import lax
from jax.sharding import PartitionSpec as P

ORDER = 12


EQUIV_RADIUS = 2.95
CHECK_RADIUS = 1.05
SOFTEN_SQ = 0.0625
FOUR_PI = 4.0 * math.pi


def with_halo(value, sides, width):
    for axis, dim in sides:
        size, length = (lax.axis_size(axis), value.shape[dim])
        up = [(i, (i + 1) % size) for i in range(size - 1)]
        down = [(j, i) for i, j in up]
        last = lax.slice_in_dim(value, length - width, length, axis=dim)
        initial = lax.slice_in_dim(value, 0, width, axis=dim)
        before = lax.ppermute(last, axis, up)
        after = lax.ppermute(initial, axis, down)
        value = jnp.concatenate([before, value, after], axis=dim)
    return value


def surface_points(edge_points):
    spacing = np.linspace(-1.0, 1.0, edge_points)
    lattice = np.stack(np.meshgrid(spacing, spacing, spacing, indexing="ij"), 0).reshape(3, -1)
    on_surface = np.max(np.abs(lattice), axis=0) > 0.999
    return lattice[:, on_surface].astype(np.float32)


def leaf_centres(leaf_index):
    coords = []
    for axis_bit in range(3):
        coord_val = jnp.zeros_like(leaf_index)
        for bit_level in range(10):
            bit_value = jnp.bitwise_and(jnp.right_shift(leaf_index, 3 * bit_level + axis_bit), 1)
            coord_val = coord_val + jnp.left_shift(bit_value, bit_level)
        coords.append(2 * coord_val + 1)
    return jnp.stack(coords, 0).astype(jnp.float32)


def transfer_kernel(octant, points):
    corner = np.array([octant & 1, octant >> 1 & 1, octant >> 2 & 1], np.float32) - 0.5
    targets = jnp.asarray(corner)[:, None] + 0.5 * CHECK_RADIUS * points
    sources = EQUIV_RADIUS * points
    separation = targets[:, :, None] - sources[:, None, :]
    return lax.rsqrt(jnp.sum(separation * separation, 0)) / FOUR_PI


def descend(upper, check_to_equiv, own_terms, points):
    checks = [
        jnp.dot(
            transfer_kernel(octant, points),
            upper,
            precision=lax.Precision.HIGHEST,
            preferred_element_type=jnp.float32,
        )
        for octant in range(8)
    ]
    stacked = jnp.stack(checks, 2).reshape(upper.shape[0], upper.shape[1] * 8)
    return (
        jnp.dot(
            check_to_equiv,
            stacked,
            precision=lax.Precision.HIGHEST,
            preferred_element_type=jnp.float32,
        )
        + own_terms
    )


def far_field(density, local_pos, points):
    sources = EQUIV_RADIUS * points
    separation = local_pos[:, None, :] - sources[:, :, None]
    inverse = lax.rsqrt(jnp.sum(separation * separation, 0))
    weighted = density * inverse / FOUR_PI
    potential = jnp.sum(weighted, 0)
    gradient = -jnp.sum(separation * (weighted * inverse * inverse)[None], 1)
    return jnp.concatenate([potential[None], gradient], 0)


def near_tile(part_pos, panel_tile):
    separation = part_pos[:, :, None] - panel_tile[:3, None, :]
    inverse = lax.rsqrt(jnp.sum(separation * separation, 0) + SOFTEN_SQ)
    weighted = panel_tile[3][None, :] * inverse / FOUR_PI
    potential = jnp.sum(weighted, 1)
    gradient = -jnp.sum(separation * (weighted * inverse * inverse)[None], 2)
    return jnp.concatenate([potential[None], gradient], 0)


def per_device(
    coarse_dens,
    owner_slot,
    check_to_equiv,
    parent_own,
    leaf_own,
    leaf_counts,
    particles,
    panels,
    near_part,
    near_pan,
    near_count,
):
    points = jnp.asarray(surface_points(ORDER))
    slots_dev = coarse_dens.shape[1]
    leaves_dev = leaf_own.shape[1]
    part_count = particles.shape[1]
    device = lax.axis_index(("grp", "box"))
    wanted = device * slots_dev + jnp.arange(slots_dev)
    slot_ids = jnp.take(owner_slot, wanted)
    gathered = lax.all_gather(coarse_dens, "box", axis=1, tiled=True)
    columns = slot_ids - lax.axis_index("grp") * gathered.shape[1]
    coarse = jnp.take(gathered, columns, axis=1)
    parents = descend(coarse, check_to_equiv, parent_own, points)
    leaves = descend(parents, check_to_equiv, leaf_own, points)
    running = jnp.cumsum(leaf_counts[0])
    part_index = jnp.arange(part_count)
    leaf_of = jnp.sum((running[:, None] <= part_index[None, :]).astype(jnp.int32), 0)
    centres = leaf_centres(device * leaves_dev + jnp.arange(leaves_dev))
    positions = particles + jnp.take(centres, leaf_of, axis=1)
    block_len = 512

    def far_block(first_row):
        leaf_ids = lax.dynamic_slice_in_dim(leaf_of, first_row, block_len)
        local_pos = lax.dynamic_slice_in_dim(particles, first_row, block_len, 1)
        return far_field(jnp.take(leaves, leaf_ids, axis=1), local_pos, points)

    firsts = jnp.arange(part_count // block_len) * block_len
    distant = lax.map(far_block, firsts).transpose(1, 0, 2).reshape(4, part_count)
    window = with_halo(panels, ((("grp", "box"), 1),), panels.shape[1])

    def tile_contrib(part_tile, window_tile):
        part_pos = lax.dynamic_slice_in_dim(positions, part_tile * 128, 128, 1)
        panel_tile = lax.dynamic_slice_in_dim(window, window_tile * 128, 128, 1)
        return near_tile(part_pos, panel_tile)

    slot_total = near_part.shape[0]

    def near_block(first_row):
        part_tiles = lax.dynamic_slice_in_dim(near_part, first_row, 8)
        window_tiles = lax.dynamic_slice_in_dim(near_pan, first_row, 8)
        return jax.vmap(tile_contrib)(part_tiles, window_tiles)

    starts = jnp.arange(slot_total // 8) * 8
    contribs = lax.map(near_block, starts).reshape(slot_total, 4, 128)
    active = (jnp.arange(slot_total) < near_count[0]).astype(jnp.float32)
    contribs = contribs * active[:, None, None]
    onehot = (near_part[:, None] == jnp.arange(part_count // 128)[None, :]).astype(jnp.float32)
    nearby = jnp.einsum("tn,tcb->cnb", onehot, contribs, precision=lax.Precision.HIGHEST).reshape(
        4, part_count
    )
    return distant + nearby


def solution(mesh):
    placed = (
        P(None, ("grp", "box")),
        P(),
        P(),
        P(None, ("grp", "box")),
        P(None, ("grp", "box")),
        P(("grp", "box"), None),
        P(None, ("grp", "box")),
        P(None, ("grp", "box")),
        P(("grp", "box")),
        P(("grp", "box")),
        P(("grp", "box")),
    )
    return jax.shard_map(
        per_device, mesh=mesh, in_specs=placed, out_specs=P(None, ("grp", "box")), check_vma=False
    )
```

profile of v0, /device:TPU:64, one launch (start us, length us, event | category | flops | bytes accessed | tf_op | source)
XLA Modules:
  0.0 556.8 jit_solution(11100674243886371253)
XLA Ops:
  0.0 3.6 collective-permute-start
  3.6 12.1 %collective-permute-start.1 = (f32[4,1024]{1,0:T(4,128)}, f32[4,1024]{1,0:T(4,128)}, u32[]{:S(2)}, u32[]{:S(2)}) collective-permute-start(f32[4,1024]{1,0:T(4,128)} %param.39), channel_id=1, source_target_pairs={{1,0},{2,1},{3,2},{4,3},{5,4},{6,5},{7,6},{8,7},{9,8},{10,9},{11,1... | collective-permute-start | bytes 49160 | tf_op jit(solution)/shard_map/ppermute | solution.py:26
  19.9 217.1 %all-gather = f32[64,1,728]{2,1,0:T(1,128)S(1)} all-gather(f32[1,1,728]{2,1,0:T(1,128)} %bitcast.177), channel_id=1, replica_groups=mesh['grp'=8,'box'=64] {'box'}, dimensions={0}, use_global_device_ids=true | all-gather | bytes 189280 | tf_op jit(solution)/shard_map/all_gather | solution.py:118
  236.9 13.9 %fusion.11 = (f32[728,728]{1,0:T(8,128)S(1)}, f32[728,728]{1,0:T(8,128)}, f32[728,728]{1,0:T(8,128)}, f32[728,728]{1,0:T(8,128)}, f32[728,728]{1,0:T(8,128)}, /*...) fusion(f32[3,728]{1,0:T(4,128)} %constant.322, f32[3,728]{1,0:T(4,128)} %constant.320, ...), kind=kLoop, calls=%fused_computation.35 | loop fusion | flops 33918976 | bytes 17038112 | tf_op jit(solution)/shard_map/reduce_sum | solution.py:54
  270.4 3.9 fusion.67
  294.4 56.7 %while.30 = (s32[]{:T(128)}, f32[4,4,512]{2,1,0:T(4,128)}, s32[4]{0:T(128)}, s32[2048]{0:T(1024)S(1)}, f32[728,64]{0,1:T(8,128)S(1)}, /*index=5*/f32[3,2048]{1,0...) while((s32[]{:T(128)}, f32[4,4,512]{2,1,0:T(4,128)}, s32[4]{0:T(128)}, ...), condition=%wide.region_22.23_spmd.clone, body=%wide.region_18.0_spmd.sunk.clone.sunk | while | flops 8578565 | bytes 13511387 | solution.py:136
  352.6 7.6 %gather_fusion.1 = f32[2048,3]{1,0:T(8,128)} fusion(f32[3,64]{0,1:T(8,128)S(1)} %copy.65, s32[2048]{0:T(1024)S(1)} %broadcast_clamp_fusion), kind=kCustom, calls=%fused_computation.1 | custom fusion | bytes 57344 | tf_op jit(solution)/shard_map/jit(_take)/gather | solution.py:127
  365.2 189.5 %while.29 = (s32[]{:T(128)}, f32[8,8,4,128]{3,2,1,0:T(4,128)S(1)}, s32[8]{0:T(128)S(1)}, s32[64]{0:T(128)S(1)}, f32[4,3072]{1,0:T(4,128)S(1)}, /*index=5*/s32[64...) while((s32[]{:T(128)}, f32[8,8,4,128]{3,2,1,0:T(4,128)S(1)}, ...), condition=%wide.region_27.28_spmd, body=%wide.region_23.27_spmd.sunk | while | flops 3017801 | bytes 2245397 | solution.py:152
  367.6 9.8 %while.31 = (s32[]{:T(128)}, f32[4,3072]{1,0:T(4,128)S(1)}, s32[8,2]{0,1:T(2,128)S(1)}, f32[8,4,128]{2,1,0:T(4,128)S(1)}, s32[]{:T(128)}) while((s32[]{:T(128)}, f32[4,3072]{1,0:T(4,128)S(1)}, s32[8,2]{0,1:T(2,128)S(1)}, f32[8,4,128]{2,1,0:T(4,128)S(1)}, s32[]{:T(128)}) %tuple.100), condition=%wide.while_cond, body=%wide.while_body.sunk | while | flops 2 | bytes 4193 | solution.py:141
  377.4 9.8 %while.32 = (s32[]{:T(128)}, f32[3,2048]{1,0:T(4,128)S(1)}, s32[8,2]{0,1:T(2,128)S(1)}, f32[8,3,128]{2,1,0:T(4,128)S(1)}, s32[]{:T(128)}) while((s32[]{:T(128)}, f32[3,2048]{1,0:T(4,128)S(1)}, s32[8,2]{0,1:T(2,128)S(1)}, f32[8,3,128]{2,1,0:T(4,128)S(1)}, s32[]{:T(128)}) %tuple.103), condition=%wide.while_cond.1, body=%wide.while_body.1.sunk | while | flops 2 | bytes 4193 | solution.py:140
  391.3 9.8 %while.31 = (s32[]{:T(128)}, f32[4,3072]{1,0:T(4,128)S(1)}, s32[8,2]{0,1:T(2,128)S(1)}, f32[8,4,128]{2,1,0:T(4,128)S(1)}, s32[]{:T(128)}) while((s32[]{:T(128)}, f32[4,3072]{1,0:T(4,128)S(1)}, s32[8,2]{0,1:T(2,128)S(1)}, f32[8,4,128]{2,1,0:T(4,128)S(1)}, s32[]{:T(128)}) %tuple.100), condition=%wide.while_cond, body=%wide.while_body.sunk | while | flops 2 | bytes 4193 | solution.py:141
  401.1 9.8 %while.32 = (s32[]{:T(128)}, f32[3,2048]{1,0:T(4,128)S(1)}, s32[8,2]{0,1:T(2,128)S(1)}, f32[8,3,128]{2,1,0:T(4,128)S(1)}, s32[]{:T(128)}) while((s32[]{:T(128)}, f32[3,2048]{1,0:T(4,128)S(1)}, s32[8,2]{0,1:T(2,128)S(1)}, f32[8,3,128]{2,1,0:T(4,128)S(1)}, s32[]{:T(128)}) %tuple.103), condition=%wide.while_cond.1, body=%wide.while_body.1.sunk | while | flops 2 | bytes 4193 | solution.py:140
  415.0 9.8 %while.31 = (s32[]{:T(128)}, f32[4,3072]{1,0:T(4,128)S(1)}, s32[8,2]{0,1:T(2,128)S(1)}, f32[8,4,128]{2,1,0:T(4,128)S(1)}, s32[]{:T(128)}) while((s32[]{:T(128)}, f32[4,3072]{1,0:T(4,128)S(1)}, s32[8,2]{0,1:T(2,128)S(1)}, f32[8,4,128]{2,1,0:T(4,128)S(1)}, s32[]{:T(128)}) %tuple.100), condition=%wide.while_cond, body=%wide.while_body.sunk | while | flops 2 | bytes 4193 | solution.py:141
  424.8 9.8 %while.32 = (s32[]{:T(128)}, f32[3,2048]{1,0:T(4,128)S(1)}, s32[8,2]{0,1:T(2,128)S(1)}, f32[8,3,128]{2,1,0:T(4,128)S(1)}, s32[]{:T(128)}) while((s32[]{:T(128)}, f32[3,2048]{1,0:T(4,128)S(1)}, s32[8,2]{0,1:T(2,128)S(1)}, f32[8,3,128]{2,1,0:T(4,128)S(1)}, s32[]{:T(128)}) %tuple.103), condition=%wide.while_cond.1, body=%wide.while_body.1.sunk | while | flops 2 | bytes 4193 | solution.py:140
  438.7 9.8 %while.31 = (s32[]{:T(128)}, f32[4,3072]{1,0:T(4,128)S(1)}, s32[8,2]{0,1:T(2,128)S(1)}, f32[8,4,128]{2,1,0:T(4,128)S(1)}, s32[]{:T(128)}) while((s32[]{:T(128)}, f32[4,3072]{1,0:T(4,128)S(1)}, s32[8,2]{0,1:T(2,128)S(1)}, f32[8,4,128]{2,1,0:T(4,128)S(1)}, s32[]{:T(128)}) %tuple.100), condition=%wide.while_cond, body=%wide.while_body.sunk | while | flops 2 | bytes 4193 | solution.py:141
  448.5 9.8 %while.32 = (s32[]{:T(128)}, f32[3,2048]{1,0:T(4,128)S(1)}, s32[8,2]{0,1:T(2,128)S(1)}, f32[8,3,128]{2,1,0:T(4,128)S(1)}, s32[]{:T(128)}) while((s32[]{:T(128)}, f32[3,2048]{1,0:T(4,128)S(1)}, s32[8,2]{0,1:T(2,128)S(1)}, f32[8,3,128]{2,1,0:T(4,128)S(1)}, s32[]{:T(128)}) %tuple.103), condition=%wide.while_cond.1, body=%wide.while_body.1.sunk | while | flops 2 | bytes 4193 | solution.py:140
  462.4 9.8 %while.31 = (s32[]{:T(128)}, f32[4,3072]{1,0:T(4,128)S(1)}, s32[8,2]{0,1:T(2,128)S(1)}, f32[8,4,128]{2,1,0:T(4,128)S(1)}, s32[]{:T(128)}) while((s32[]{:T(128)}, f32[4,3072]{1,0:T(4,128)S(1)}, s32[8,2]{0,1:T(2,128)S(1)}, f32[8,4,128]{2,1,0:T(4,128)S(1)}, s32[]{:T(128)}) %tuple.100), condition=%wide.while_cond, body=%wide.while_body.sunk | while | flops 2 | bytes 4193 | solution.py:141
  472.2 9.8 %while.32 = (s32[]{:T(128)}, f32[3,2048]{1,0:T(4,128)S(1)}, s32[8,2]{0,1:T(2,128)S(1)}, f32[8,3,128]{2,1,0:T(4,128)S(1)}, s32[]{:T(128)}) while((s32[]{:T(128)}, f32[3,2048]{1,0:T(4,128)S(1)}, s32[8,2]{0,1:T(2,128)S(1)}, f32[8,3,128]{2,1,0:T(4,128)S(1)}, s32[]{:T(128)}) %tuple.103), condition=%wide.while_cond.1, body=%wide.while_body.1.sunk | while | flops 2 | bytes 4193 | solution.py:140
  486.0 9.8 %while.31 = (s32[]{:T(128)}, f32[4,3072]{1,0:T(4,128)S(1)}, s32[8,2]{0,1:T(2,128)S(1)}, f32[8,4,128]{2,1,0:T(4,128)S(1)}, s32[]{:T(128)}) while((s32[]{:T(128)}, f32[4,3072]{1,0:T(4,128)S(1)}, s32[8,2]{0,1:T(2,128)S(1)}, f32[8,4,128]{2,1,0:T(4,128)S(1)}, s32[]{:T(128)}) %tuple.100), condition=%wide.while_cond, body=%wide.while_body.sunk | while | flops 2 | bytes 4193 | solution.py:141
  495.8 9.8 %while.32 = (s32[]{:T(128)}, f32[3,2048]{1,0:T(4,128)S(1)}, s32[8,2]{0,1:T(2,128)S(1)}, f32[8,3,128]{2,1,0:T(4,128)S(1)}, s32[]{:T(128)}) while((s32[]{:T(128)}, f32[3,2048]{1,0:T(4,128)S(1)}, s32[8,2]{0,1:T(2,128)S(1)}, f32[8,3,128]{2,1,0:T(4,128)S(1)}, s32[]{:T(128)}) %tuple.103), condition=%wide.while_cond.1, body=%wide.while_body.1.sunk | while | flops 2 | bytes 4193 | solution.py:140
  509.7 9.8 %while.31 = (s32[]{:T(128)}, f32[4,3072]{1,0:T(4,128)S(1)}, s32[8,2]{0,1:T(2,128)S(1)}, f32[8,4,128]{2,1,0:T(4,128)S(1)}, s32[]{:T(128)}) while((s32[]{:T(128)}, f32[4,3072]{1,0:T(4,128)S(1)}, s32[8,2]{0,1:T(2,128)S(1)}, f32[8,4,128]{2,1,0:T(4,128)S(1)}, s32[]{:T(128)}) %tuple.100), condition=%wide.while_cond, body=%wide.while_body.sunk | while | flops 2 | bytes 4193 | solution.py:141
  519.5 9.8 %while.32 = (s32[]{:T(128)}, f32[3,2048]{1,0:T(4,128)S(1)}, s32[8,2]{0,1:T(2,128)S(1)}, f32[8,3,128]{2,1,0:T(4,128)S(1)}, s32[]{:T(128)}) while((s32[]{:T(128)}, f32[3,2048]{1,0:T(4,128)S(1)}, s32[8,2]{0,1:T(2,128)S(1)}, f32[8,3,128]{2,1,0:T(4,128)S(1)}, s32[]{:T(128)}) %tuple.103), condition=%wide.while_cond.1, body=%wide.while_body.1.sunk | while | flops 2 | bytes 4193 | solution.py:140
  533.4 9.8 %while.31 = (s32[]{:T(128)}, f32[4,3072]{1,0:T(4,128)S(1)}, s32[8,2]{0,1:T(2,128)S(1)}, f32[8,4,128]{2,1,0:T(4,128)S(1)}, s32[]{:T(128)}) while((s32[]{:T(128)}, f32[4,3072]{1,0:T(4,128)S(1)}, s32[8,2]{0,1:T(2,128)S(1)}, f32[8,4,128]{2,1,0:T(4,128)S(1)}, s32[]{:T(128)}) %tuple.100), condition=%wide.while_cond, body=%wide.while_body.sunk | while | flops 2 | bytes 4193 | solution.py:141
  543.2 9.8 %while.32 = (s32[]{:T(128)}, f32[3,2048]{1,0:T(4,128)S(1)}, s32[8,2]{0,1:T(2,128)S(1)}, f32[8,3,128]{2,1,0:T(4,128)S(1)}, s32[]{:T(128)}) while((s32[]{:T(128)}, f32[3,2048]{1,0:T(4,128)S(1)}, s32[8,2]{0,1:T(2,128)S(1)}, f32[8,3,128]{2,1,0:T(4,128)S(1)}, s32[]{:T(128)}) %tuple.103), condition=%wide.while_cond.1, body=%wide.while_body.1.sunk | while | flops 2 | bytes 4193 | solution.py:140
  (617 shorter events, 273.9 us)
Async XLA Ops:
  0.0 268.5 %copy-start = (f32[728,728]{1,0:T(8,128)S(1)}, f32[728,728]{1,0:T(8,128)}, u32[]{:S(2)}) copy-start(f32[728,728]{1,0:T(8,128)} %param.34) | copy-start | bytes 6359812
  0.0 364.4 %collective-permute-start = (f32[4,1024]{1,0:T(4,128)}, f32[4,1024]{1,0:T(4,128)}, u32[]{:S(2)}, u32[]{:S(2)}) collective-permute-start(f32[4,1024]{1,0:T(4,128)} %param.39), channel_id=1, source_target_pairs={{0,1},{1,2},{2,3},{3,4},{4,5},{5,6},{6,7},{7,8},{8,9},{9,10},{10,1... | collective-permute-start | bytes 49160 | tf_op jit(solution)/shard_map/ppermute | solution.py:25
  3.6 360.8 %collective-permute-start.1 = (f32[4,1024]{1,0:T(4,128)}, f32[4,1024]{1,0:T(4,128)}, u32[]{:S(2)}, u32[]{:S(2)}) collective-permute-start(f32[4,1024]{1,0:T(4,128)} %param.39), channel_id=1, source_target_pairs={{1,0},{2,1},{3,2},{4,3},{5,4},{6,5},{7,6},{8,7},{9,8},{10,9},{11,1... | collective-permute-start | bytes 49160 | tf_op jit(solution)/shard_map/ppermute | solution.py:26
  250.9 4.3 copy-start.3
  250.9 4.3 copy-start.5
  253.0 4.4 copy-start.7
  255.2 4.3 copy-start.9
  257.4 4.3 copy-start.11
  259.5 4.3 copy-start.13
  261.7 4.3 copy-start.15
  263.9 4.6 copy-start.19
  268.5 5.9 %copy-start.14 = (f32[728,728]{1,0:T(8,128)S(1)}, f32[728,728]{1,0:T(8,128)}, u32[]{:S(2)}) copy-start(f32[728,728]{1,0:T(8,128)} %get-tuple-element.176) | copy-start | bytes 6359812
  270.4 6.1 %copy-start.12 = (f32[728,728]{1,0:T(8,128)S(1)}, f32[728,728]{1,0:T(8,128)}, u32[]{:S(2)}) copy-start(f32[728,728]{1,0:T(8,128)} %get-tuple-element.177) | copy-start | bytes 6359812
  274.4 4.3 copy-start.10
  276.5 4.3 copy-start.8
  278.7 4.3 copy-start.6
  280.8 4.6 copy-start.4
  283.0 4.6 copy-start.2
  285.4 5.0 copy-start.23
  285.4 5.5 copy-start.18
  352.6 11.8 %copy-start.21 = (f32[4,1024]{1,0:T(4,128)S(1)}, f32[4,1024]{1,0:T(4,128)}, u32[]{:S(2)}) copy-start(f32[4,1024]{1,0:T(4,128)} %param.39) | copy-start | bytes 49156
  360.2 5.0 copy-start.20
  360.2 5.0 copy-start.22
  360.2 5.0 copy-start.24
  (3 other events, 8.9 us)
where the time goes:
time: 568 us; the launch traced here: 557 us
  blocking collectives  217 us (38%)
  local copies, waits for them, and re-layouts  201 us (35%)
  other arithmetic  56.5 us (10%)
  matrix products  41.9 us (7%)
  loops' own time  22.7 us (4%)
  starting transfers between devices  15.7 us (3%)
    all_gather x1, blocking collectives, per_device(): gathered = lax.all_gather(coarse_dens, 'box', axis=1, tiled=True)  217 us
    gather x384, local copies, waits for them, and re-layouts  156 us
    dot_general x16, matrix products, descend(): jnp.dot(transfer_kernel(octant, points), upper, precision=lax.Precision.H...  36.7 us
    gather x8, local copies, waits for them, and re-layouts, far_block(): return far_field(jnp.take(leaves, leaf_ids, axis=1), local_pos, points)  22.5 us
    another operation x1, loops' own time, per_device(): contribs = lax.map(near_block, starts).reshape(slot_total, 4, 128)  14 us
    reduce_sum x1, other arithmetic, transfer_kernel(): return lax.rsqrt(jnp.sum(separation * separation, 0)) / FOUR_PI  13.9 us
    ppermute x1, starting transfers between devices, with_halo(): after = lax.ppermute(initial, axis, down)  12.1 us
  transfers between devices with their start and end apart: 2, of which 0 were waited for; matrix products, arithmetic and copies ran while one was open for 22% of the time, Pallas kernels for 0%

commit v1 on v0

v1 whole, which is shorter than its diff:
```python
import functools
import math

import jax
import jax.numpy as jnp
import ml_dtypes
import numpy as np
from jax import lax
from jax.experimental import pallas as pl
from jax.experimental.pallas import tpu as pltpu
from jax.sharding import PartitionSpec as P

ORDER = 12
EQUIV_RADIUS = 2.95
CHECK_RADIUS = 1.05
SOFTEN_SQ = 0.0625
FOUR_PI = 4.0 * math.pi
MESH = pl.DeviceIdType.MESH

NPTS = 728
MAGS = 91
BLK = 96
WID = 8 * BLK
F32, BF16 = jnp.float32, jnp.bfloat16


def surface_points(edge_points):
    spacing = np.linspace(-1.0, 1.0, edge_points)
    lattice = np.stack(np.meshgrid(spacing, spacing, spacing, indexing="ij"), 0).reshape(3, -1)
    on_surface = np.max(np.abs(lattice), axis=0) > 0.999
    return lattice[:, on_surface].astype(np.float32)


def split2(value):
    hi = value.astype(ml_dtypes.bfloat16)
    lo = (value - hi.astype(np.float32)).astype(ml_dtypes.bfloat16)
    return hi, lo


@functools.lru_cache(maxsize=None)
def tables():
    points = surface_points(ORDER).astype(np.float64)
    grid = np.rint((points + 1.0) * (ORDER - 1) / 2.0).astype(int)
    index = {tuple(g): i for i, g in enumerate(grid.T)}
    half = ORDER // 2
    mags = [g for g in grid.T if min(g) >= half]
    order = np.full(WID, -1)
    for s in range(8):
        for m, g in enumerate(mags):
            key = tuple(g[a] if s >> a & 1 else ORDER - 1 - g[a] for a in range(3))
            order[BLK * s + m] = index[key]
    live = order >= 0
    placed = points[:, np.where(live, order, 0)]
    targets = -0.5 + 0.5 * CHECK_RADIUS * placed
    separation = targets[:, :, None] - EQUIV_RADIUS * placed[:, None, :]
    k0 = 1.0 / (FOUR_PI * np.sqrt(np.sum(separation * separation, 0)))
    k0 = np.where(live[:, None] & live[None, :], k0, 0.0).astype(np.float32)
    k_pair = np.concatenate(split2(k0), 1)
    perm = np.zeros((WID, WID), np.float32)
    perm[np.nonzero(live)[0], order[live]] = 1.0
    size = np.ones((3, BLK))
    size[:, :MAGS] = np.array([[points[a, index[tuple(g)]] for g in mags] for a in range(3)])
    rows = np.concatenate([2.0 * EQUIV_RADIUS * size, EQUIV_RADIUS**2 * np.sum(size * size, 0)[None]], 0)
    mag = np.broadcast_to(rows.astype(np.float32)[:, :, None], (4, BLK, 128)).copy()
    return k_pair, perm.astype(ml_dtypes.bfloat16), perm.T.copy().astype(ml_dtypes.bfloat16), mag


def device_index():
    return lax.axis_index("grp") * 64 + lax.axis_index("box")


def comm_kernel(
    owner_ref, coarse_ref, panels_ref, coarse_out, win_out, line, picked, crossed, win,
    send1, recv1, send2, recv2, send3, recv3,
):
    grp, box = lax.axis_index("grp"), lax.axis_index("box")
    row, col = box // 8, box % 8
    me = grp * 64 + box
    nxt, prv = lax.rem(me + 1, 512), lax.rem(me + 511, 512)
    cols = [row * 8 + lax.rem(col + r, 8) for r in range(1, 8)]
    rows = [lax.rem(row + r, 8) * 8 + col for r in range(1, 8)]
    beside = [(nxt // 64, nxt % 64), (prv // 64, prv % 64)]

    barrier = pltpu.get_barrier_semaphore()
    for other in cols + rows:
        pl.semaphore_signal(barrier, inc=1, device_id=(grp, other), device_id_type=MESH)
    for other in beside:
        pl.semaphore_signal(barrier, inc=1, device_id=other, device_id_type=MESH)
    line[col] = jnp.zeros((8, 128), F32)
    for r in range(6):
        width = min(128, NPTS - 128 * r)
        line[col, r : r + 1, 0:width] = coarse_ref[0:1, 128 * r : 128 * r + width]
    win[1] = panels_ref[...]
    pl.semaphore_wait(barrier, 16)

    first = []
    for r in range(1, 8):
        first.append(
            pltpu.make_async_remote_copy(
                src_ref=line.at[col], dst_ref=line.at[col], send_sem=send1.at[r - 1], recv_sem=recv1.at[r - 1],
                device_id=(grp, cols[r - 1]), device_id_type=MESH,
            )
        )
        first[-1].start()
    halo = []
    for r, other in enumerate(beside):
        halo.append(
            pltpu.make_async_remote_copy(
                src_ref=win.at[1], dst_ref=win.at[2 * r], send_sem=send3.at[r], recv_sem=recv3.at[r],
                device_id=other, device_id_type=MESH,
            )
        )
        halo[-1].start()
    for copy in first:
        copy.wait()
    for r in range(8):
        there = lax.rem(row + r, 8) * 8 + col
        want = jnp.bitwise_and(owner_ref[grp * 64 + there], 7)
        if r == 0:
            crossed[row] = line[want]
        else:
            picked[r] = line[want]
    second = []
    for r in range(1, 8):
        second.append(
            pltpu.make_async_remote_copy(
                src_ref=picked.at[r], dst_ref=crossed.at[row], send_sem=send2.at[r - 1], recv_sem=recv2.at[r - 1],
                device_id=(grp, rows[r - 1]), device_id_type=MESH,
            )
        )
        second[-1].start()
    for copy in halo:
        copy.wait()
    keep_low = jnp.where(me == 0, 0.0, 1.0)
    keep_high = jnp.where(me == 511, 0.0, 1.0)
    win_out[0] = win[0] * keep_low
    win_out[1] = win[1]
    win_out[2] = win[2] * keep_high
    for copy in second:
        copy.wait()
    slot = jnp.bitwise_and(owner_ref[me], 63)
    coarse_out[...] = crossed[jnp.right_shift(slot, 3)]


def exchange(owner_slot, coarse_row, panels):
    vmem = pl.BlockSpec(memory_space=pltpu.VMEM)
    return pl.pallas_call(
        comm_kernel,
        out_shape=(jax.ShapeDtypeStruct((8, 128), F32), jax.ShapeDtypeStruct((3, 4, 1024), F32)),
        in_specs=[pl.BlockSpec(memory_space=pltpu.SMEM), vmem, vmem],
        out_specs=(vmem, vmem),
        scratch_shapes=[
            pltpu.VMEM((8, 8, 128), F32),
            pltpu.VMEM((8, 8, 128), F32),
            pltpu.VMEM((8, 8, 128), F32),
            pltpu.VMEM((3, 4, 1024), F32),
            pltpu.SemaphoreType.DMA((7,)),
            pltpu.SemaphoreType.DMA((7,)),
            pltpu.SemaphoreType.DMA((7,)),
            pltpu.SemaphoreType.DMA((7,)),
            pltpu.SemaphoreType.DMA((2,)),
            pltpu.SemaphoreType.DMA((2,)),
        ],
        compiler_params=pltpu.CompilerParams(collective_id=0, has_side_effects=True),
        name="exchange",
    )(owner_slot, coarse_row, panels)


def pieces3(value):
    hi = value.astype(BF16).astype(F32)
    rest = value - hi
    mid = rest.astype(BF16).astype(F32)
    return hi, mid, (rest - mid).astype(BF16).astype(F32)


def mm(a, b):
    return jnp.dot(a, b, preferred_element_type=F32)


def compute_kernel(
    device_ref, part_s, pan_s, count_s, coarse_ref, m_ref, pown_ref, lown_ref, leaf_counts_ref, parts_ref, win_ref,
    k_ref, perm_ref, permt_ref, mag_ref, out_ref,
    m_full, m_pair, turn, pown, lown, hot, xrel, xf, xk, pf, pk, zb, acc, uexp,
):
    lane = lax.broadcasted_iota(jnp.int32, (1, 128), 1)
    device = device_ref[0]

    counts = leaf_counts_ref[...].astype(F32)
    g_row = lax.broadcasted_iota(jnp.int32, (64, 64), 0)
    g_col = lax.broadcasted_iota(jnp.int32, (64, 64), 1)
    upto = jnp.sum(jnp.where(g_col <= g_row, counts, 0.0), 1, keepdims=True)
    before = jnp.sum(jnp.where(g_col < g_row, counts, 0.0), 1, keepdims=True)
    leaf = lax.broadcasted_iota(jnp.int32, (64, 1), 0)
    local = []
    for a in range(3):
        c = jnp.bitwise_and(jnp.right_shift(leaf, a), 1) + 2 * jnp.bitwise_and(jnp.right_shift(leaf, 3 + a), 1)
        local.append((2 * c - 3).astype(F32))
    for n in range(16):
        index = (lax.broadcasted_iota(jnp.int32, (1, 128), 1) + 128 * n).astype(F32)
        inside = jnp.where((index >= before) & (index < upto), 1.0, 0.0)
        hot[n, 0:64] = inside.astype(BF16)
        hot[n, 64:128] = inside.astype(BF16)
        for a in range(3):
            centre = jnp.sum(inside * local[a], 0, keepdims=True)
            xrel[a : a + 1, 128 * n : 128 * n + 128] = parts_ref[a : a + 1, 128 * n : 128 * n + 128] + centre

    xf[...] = jnp.zeros_like(xf)
    pf[...] = jnp.zeros_like(pf)
    x = xrel[0:3, :]
    hi, mid, low = pieces3(x)
    for r, piece in enumerate((hi, mid, hi, low, hi, mid)):
        xf[3 * r : 3 * r + 3, :] = piece
    for r, piece in enumerate(pieces3(jnp.sum(x * x, 0, keepdims=True))):
        xf[18 + r : 19 + r, :] = piece
    xf[21:24, :] = jnp.ones((3, 2048), F32)
    for n in range(16):
        xk[n] = xf[:, 128 * n : 128 * n + 128].astype(BF16)
    axis = lax.broadcasted_iota(jnp.int32, (4, 1), 0)
    shift = jnp.zeros((4, 1), jnp.int32)
    for b in range(3):
        bit = jnp.bitwise_and(jnp.right_shift(device, 3 * b + axis), 1)
        shift = shift + jnp.left_shift(bit, b)
    centre = jnp.where(axis < 3, (8 * shift + 4).astype(F32), 0.0)
    for s in range(3):
        raw = win_ref[s] - centre
        at = slice(1024 * s, 1024 * s + 1024)
        z = raw[0:3]
        hi, mid, low = pieces3(z)
        for r, piece in enumerate((hi, hi, mid, hi, low, mid)):
            pf[3 * r : 3 * r + 3, at] = -2.0 * piece
        pf[18:21, at] = jnp.ones((3, 1024), F32)
        for r, piece in enumerate(pieces3(jnp.sum(z * z, 0, keepdims=True) + SOFTEN_SQ)):
            pf[21 + r : 22 + r, at] = piece
        pf[24:28, at] = raw

    def panel_tile(t, carry):
        block = pf[:, pl.ds(pl.multiple_of(t * 128, 128), 128)]
        turned = block.T
        pk[t] = turned[:, 0:32].astype(BF16)
        for a in range(4):
            zb[t, a] = jnp.broadcast_to(turned[:, 24 + a : 25 + a], (128, 128))
        return carry

    lax.fori_loop(0, 24, panel_tile, 0)

    acc[...] = jnp.zeros_like(acc)

    def near_slot(t, carry):
        to, tile = part_s[t], pan_s[t]
        r2 = mm(pk[tile], xk[to])
        sums = [jnp.zeros((8, 128), F32)] * 5
        for v in range(16):
            rows = slice(8 * v, 8 * v + 8)
            inv = lax.rsqrt(r2[rows])
            w = zb[tile, 3, rows] * inv
            w3 = w * (inv * inv)
            sums[0] = sums[0] + w
            sums[1] = sums[1] + w3
            for a in range(3):
                sums[2 + a] = sums[2 + a] + w3 * zb[tile, a, rows]
        for q in range(5):
            acc[to, q] += sums[q]
        return carry

    lax.fori_loop(0, count_s[0], near_slot, 0)

    m_full[NPTS:WID, :] = jnp.zeros((WID - NPTS, WID), F32)
    m_full[:, 640:WID] = jnp.zeros((WID, 128), F32)

    def m_copy(r, carry):
        rows = pl.ds(pl.multiple_of(r * 56, 8), 56)
        m_full[rows, 0:NPTS] = m_ref[rows, :]
        return carry

    lax.fori_loop(0, 13, m_copy, 0)

    def m_split(r, carry):
        rows = pl.ds(pl.multiple_of(r * 64, 64), 64)
        value = m_full[rows, :]
        hi = value.astype(BF16)
        m_pair[rows, 0:WID] = hi
        m_pair[rows, WID : 2 * WID] = (value - hi.astype(F32)).astype(BF16)
        return carry

    lax.fori_loop(0, 12, m_split, 0)

    turn[:, 640:WID] = jnp.zeros((128, 128), F32)
    for k in range(8):
        value = jnp.broadcast_to(pown_ref[k : k + 1, :], (8, NPTS))
        turn[8 * k : 8 * k + 8, 0:NPTS] = value
        turn[64 + 8 * k : 72 + 8 * k, 0:NPTS] = value
    pown[...] = turn[...].T
    turn[0:64, 0:NPTS] = lown_ref[...]
    turn[64:128, 0:NPTS] = lown_ref[...]
    lown[...] = turn[...].T

    low_half = lane < 64
    column = jnp.bitwise_and(lane, 63)

    def swapped(value, octant):
        blocks = [value[BLK * s : BLK * s + BLK] for s in range(8)]
        for b in range(3):
            mask = jnp.bitwise_and(jnp.right_shift(octant, b), 1) == 1
            blocks = [jnp.where(mask, blocks[s ^ (1 << b)], blocks[s]) for s in range(8)]
        return jnp.concatenate(blocks, 0)

    def pieces(value):
        hi = value.astype(BF16).astype(F32)
        return jnp.where(low_half, hi, value - hi).astype(BF16)

    def both(pair_ref, x2):
        product = mm(pair_ref[:, 0:WID], x2) + mm(pair_ref[:, WID : 2 * WID], x2)
        return product + pltpu.roll(product, 64, 1)

    def level(x2, octant, own):
        placed = swapped(x2, octant).astype(BF16)
        checks = swapped(both(k_ref, placed), octant)
        back = mm(permt_ref[...], pieces(checks)).astype(BF16)
        return both(m_pair, back) + own

    rows_hi, rows_lo = [], []
    row = lax.broadcasted_iota(jnp.int32, (128, 1), 0)
    spread = []
    for r in range(6):
        value = coarse_ref[r : r + 1, :]
        hi = value.astype(BF16).astype(F32)
        spread.append(jnp.where(row < 64, hi, value - hi))
    spread = jnp.concatenate(spread, 1).astype(BF16)
    start = lax.dot_general(perm_ref[...], spread, (((1,), (1,)), ((), ())), preferred_element_type=F32)
    parents = level(start, jnp.right_shift(column, 3), pown[...])
    placed = mm(perm_ref[...], pieces(parents))
    leaves = level(placed, jnp.bitwise_and(column, 7), lown[...])
    dens = mm(perm_ref[...], pieces(leaves)).astype(BF16)

    def far_tile(n, carry):
        uexp[...] = mm(dens, hot[n])
        at = pl.ds(pl.multiple_of(n * 128, 128), 128)
        y = [jnp.broadcast_to(parts_ref[a : a + 1, at], (8, 128)) for a in range(3)]
        y2 = y[0] * y[0] + y[1] * y[1] + y[2] * y[2]
        pot = jnp.zeros((8, 128), F32)
        total = [jnp.zeros((8, 128), F32)] * 4
        for v in range(BLK // 8):
            rows = slice(8 * v, 8 * v + 8)
            mags = [mag_ref[a, rows] for a in range(3)]
            part = [y2 + mag_ref[3, rows]]
            for a in range(3):
                step = y[a] * mags[a]
                part = [q + step for q in part] + [q - step for q in part]
            w3 = []
            for s in range(8):
                inv = lax.rsqrt(part[s])
                w = uexp[BLK * s + 8 * v : BLK * s + 8 * v + 8] * inv
                pot = pot + w
                w3.append(w * (inv * inv))
            x0 = [w3[s] + w3[s + 1] for s in (0, 2, 4, 6)]
            x1 = [w3[s + 1] - w3[s] for s in (0, 2, 4, 6)]
            y0 = [x0[s] + x0[s + 1] for s in (0, 2)]
            y1 = [x0[s + 1] - x0[s] for s in (0, 2)]
            total[0] = total[0] + (y0[0] + y0[1])
            total[1] = total[1] + ((x1[0] + x1[1]) + (x1[2] + x1[3])) * mags[0]
            total[2] = total[2] + (y1[0] + y1[1]) * mags[1]
            total[3] = total[3] + (y0[1] - y0[0]) * mags[2]
        near = [acc[n, q] for q in range(5)]
        scale = 1.0 / FOUR_PI
        out_ref[0:1, at] = scale * jnp.sum(pot + near[0], 0, keepdims=True)
        for a in range(3):
            whole = (y[a] * total[0] - 0.5 * total[1 + a]) + (xrel[a : a + 1, at] * near[1] - near[2 + a])
            out_ref[1 + a : 2 + a, at] = -scale * jnp.sum(whole, 0, keepdims=True)
        return carry

    lax.fori_loop(0, 16, far_tile, 0)


def evaluate(device, near_part, near_pan, near_count, coarse, m, pown, lown, leaf_counts, particles, window):
    vmem = pl.BlockSpec(memory_space=pltpu.VMEM)
    smem = pl.BlockSpec(memory_space=pltpu.SMEM)
    constants = [jnp.asarray(value) for value in tables()]
    return pl.pallas_call(
        compute_kernel,
        out_shape=jax.ShapeDtypeStruct((4, 2048), F32),
        in_specs=[smem] * 4 + [vmem] * 11,
        out_specs=vmem,
        scratch_shapes=[
            pltpu.VMEM((WID, WID), F32),
            pltpu.VMEM((WID, 2 * WID), BF16),
            pltpu.VMEM((128, WID), F32),
            pltpu.VMEM((WID, 128), F32),
            pltpu.VMEM((WID, 128), F32),
            pltpu.VMEM((16, 128, 128), BF16),
            pltpu.VMEM((8, 2048), F32),
            pltpu.VMEM((32, 2048), F32),
            pltpu.VMEM((16, 32, 128), BF16),
            pltpu.VMEM((128, 3072), F32),
            pltpu.VMEM((24, 128, 32), BF16),
            pltpu.VMEM((24, 4, 128, 128), F32),
            pltpu.VMEM((16, 5, 8, 128), F32),
            pltpu.VMEM((WID, 128), F32),
        ],
        compiler_params=pltpu.CompilerParams(vmem_limit_bytes=48 * 1024 * 1024),
        name="evaluate",
    )(device, near_part, near_pan, near_count, coarse, m, pown, lown, leaf_counts, particles, window, *constants)


def per_device(
    coarse_dens, owner_slot, check_to_equiv, parent_own, leaf_own, leaf_counts, particles, panels, near_part,
    near_pan, near_count,
):
    coarse, window = exchange(owner_slot, coarse_dens.T, panels)
    device = device_index().reshape(1)
    return evaluate(
        device, near_part, near_pan, near_count, coarse, check_to_equiv, parent_own.T, leaf_own.T, leaf_counts,
        particles, window,
    )


def solution(mesh):
    both = ("grp", "box")
    placed = (
        P(None, both), P(), P(), P(None, both), P(None, both), P(both, None), P(None, both), P(None, both), P(both),
        P(both), P(both),
    )
    return jax.shard_map(per_device, mesh=mesh, in_specs=placed, out_specs=P(None, both), check_vma=False)
```

time: 568 us -> 67.3 us (0.12)
  the two profiles are of different devices: /device:TPU:64 before, /device:TPU:2 now
where the time goes in v1:
time: 67.3 us; the launch traced here: 66.6 us
  Pallas kernels  55 us (82%)
  local copies, waits for them, and re-layouts  10.9 us (16%)
  between operations  0.68 us (1%)
    pallas_call x1, Pallas kernels, evaluate(): pl.pallas_call(compute_kernel, out_shape=jax.ShapeDtypeStruct((4, 2048),...  31.2 us
    pallas_call x1, Pallas kernels, exchange(): pl.pallas_call(comm_kernel, out_shape=(jax.ShapeDtypeStruct((8, 128), F32...  23.8 us
    unnamed x24, local copies, waits for them, and re-layouts  10.9 us

profile of v1, /device:TPU:2, one launch (start us, length us, event | category | flops | bytes accessed | tf_op | source)
XLA Modules:
  0.0 66.6 jit_solution(15162239679528715576)
XLA Ops:
  0.7 23.8 %exchange.1 = (f32[8,128]{1,0:T(8,128)}, f32[3,4,1024]{2,1,0:T(4,128)}) custom-call(s32[512]{0:T(512)} %owner_ref.1, f32[1,728]{1,0:T(1,128)} %bitcast.6, f32[4,1024]{1,0:T(4,128)} %panels_ref.1), custom_call_target="tpu_custom_call" | custom-call | tf_op jit(solution)/shard_map/exchange/pallas_call | solution.py:147
  24.4 0.0 copy-start
  24.5 1.6 %copy-done = f32[728,728]{1,0:T(8,128)S(1)} copy-done((f32[728,728]{1,0:T(8,128)S(1)}, f32[728,728]{1,0:T(8,128)}, u32[]{:S(2)}) %copy-start) | copy-done | bytes 2119960
  26.1 0.0 copy-start.1
  26.1 1.3 %copy-done.1 = bf16[768,768]{1,0:T(8,128)(2,1)S(1)} copy-done((bf16[768,768]{1,0:T(8,128)(2,1)S(1)}, bf16[768,768]{1,0:T(8,128)(2,1)}, u32[]{:S(2)}) %copy-start.1) | copy-done | bytes 1179672
  27.3 0.0 copy-start.2
  27.3 1.3 %copy-done.2 = bf16[768,768]{1,0:T(8,128)(2,1)S(1)} copy-done((bf16[768,768]{1,0:T(8,128)(2,1)S(1)}, bf16[768,768]{1,0:T(8,128)(2,1)}, u32[]{:S(2)}) %copy-start.2) | copy-done | bytes 1179672
  28.6 0.0 copy-start.3
  28.6 0.9 %copy-done.3 = f32[728,64]{0,1:T(8,128)S(1)} copy-done((f32[728,64]{0,1:T(8,128)S(1)}, f32[728,64]{0,1:T(8,128)}, u32[]{:S(2)}) %copy-start.3) | copy-done | bytes 186392
  29.5 0.0 copy-start.4
  29.5 0.9 %copy-done.4 = f32[4,96,128]{2,1,0:T(8,128)S(1)} copy-done((f32[4,96,128]{2,1,0:T(8,128)S(1)}, f32[4,96,128]{2,1,0:T(8,128)}, u32[]{:S(2)}) %copy-start.4) | copy-done | bytes 196632
  30.5 0.0 copy-start.5
  30.5 0.8 %copy-done.5 = f32[3,4,1024]{2,1,0:T(4,128)S(1)} copy-done((f32[3,4,1024]{2,1,0:T(4,128)S(1)}, f32[3,4,1024]{2,1,0:T(4,128)}, u32[]{:S(2)}) %copy-start.5) | copy-done | bytes 49176
  31.3 0.0 copy-start.6
  31.3 0.8 %copy-done.6 = f32[3,2048]{1,0:T(4,128)S(1)} copy-done((f32[3,2048]{1,0:T(4,128)S(1)}, f32[3,2048]{1,0:T(4,128)}, u32[]{:S(2)}) %copy-start.6) | copy-done | bytes 24600
  32.0 0.0 copy-start.7
  32.0 0.7 %copy-done.7 = f32[728,8]{0,1:T(8,128)S(1)} copy-done((f32[728,8]{0,1:T(8,128)S(1)}, f32[728,8]{0,1:T(8,128)}, u32[]{:S(2)}) %copy-start.7) | copy-done | bytes 23320
  32.8 0.0 copy-start.8
  32.8 0.7 %copy-done.8 = f32[8,128]{1,0:T(8,128)S(1)} copy-done((f32[8,128]{1,0:T(8,128)S(1)}, f32[8,128]{1,0:T(8,128)}, u32[]{:S(2)}) %copy-start.8) | copy-done | bytes 4120
  33.4 0.0 copy-start.9
  33.4 0.7 copy-done.9
  34.1 0.7 copy-done.10
  34.8 0.7 copy-done.11
  35.4 31.2 %evaluate.1 = f32[4,2048]{1,0:T(4,128)} custom-call(s32[1]{0:T(128)} %bitcast.device_ref, s32[64]{0:T(128)S(1)} %copy-done.9, s32[64]{0:T(128)S(1)} %copy-done.10, s32[1]{0:T(128)S(6)} %copy.16.count_s, f32[8,128]{1,0:T(8,128)S(1)} %copy-done.8, f32[728,728]{1,0:T(8,128)S(1)} %copy-done, f32[8,728]{1,0:T(8,128)S(1)} %bitcast.5, f32[64,728]{1,0:T(8,128)S(1)} %bitcast.4, ...), custom_call_target="tpu_custom_call" | custom-call | tf_op jit(solution)/shard_map/evaluate/pallas_call | solution.py:378
  (2 shorter events, 0.0 us)
Async XLA Ops:
  24.4 1.6 %copy-start = (f32[728,728]{1,0:T(8,128)S(1)}, f32[728,728]{1,0:T(8,128)}, u32[]{:S(2)}) copy-start(f32[728,728]{1,0:T(8,128)} %m_ref.1) | copy-start | bytes 6359812
  26.1 1.3 %copy-start.1 = (bf16[768,768]{1,0:T(8,128)(2,1)S(1)}, bf16[768,768]{1,0:T(8,128)(2,1)}, u32[]{:S(2)}) copy-start(bf16[768,768]{1,0:T(8,128)(2,1)} %constant.21.clone.permt_ref) | copy-start | bytes 3538948
  27.3 1.3 %copy-start.2 = (bf16[768,768]{1,0:T(8,128)(2,1)S(1)}, bf16[768,768]{1,0:T(8,128)(2,1)}, u32[]{:S(2)}) copy-start(bf16[768,768]{1,0:T(8,128)(2,1)} %constant.20.clone.perm_ref) | copy-start | bytes 3538948
  28.6 0.9 %copy-start.3 = (f32[728,64]{0,1:T(8,128)S(1)}, f32[728,64]{0,1:T(8,128)}, u32[]{:S(2)}) copy-start(f32[728,64]{0,1:T(8,128)} %param.19) | copy-start | bytes 559108
  29.5 0.9 %copy-start.4 = (f32[4,96,128]{2,1,0:T(8,128)S(1)}, f32[4,96,128]{2,1,0:T(8,128)}, u32[]{:S(2)}) copy-start(f32[4,96,128]{2,1,0:T(8,128)} %constant.22.clone.mag_ref) | copy-start | bytes 589828
  30.5 0.8 %copy-start.5 = (f32[3,4,1024]{2,1,0:T(4,128)S(1)}, f32[3,4,1024]{2,1,0:T(4,128)}, u32[]{:S(2)}) copy-start(f32[3,4,1024]{2,1,0:T(4,128)} %get-tuple-element.8.win_ref) | copy-start | bytes 147460
  31.3 0.8 %copy-start.6 = (f32[3,2048]{1,0:T(4,128)S(1)}, f32[3,2048]{1,0:T(4,128)}, u32[]{:S(2)}) copy-start(f32[3,2048]{1,0:T(4,128)} %parts_ref.1) | copy-start | bytes 73732
  32.0 0.7 %copy-start.7 = (f32[728,8]{0,1:T(8,128)S(1)}, f32[728,8]{0,1:T(8,128)}, u32[]{:S(2)}) copy-start(f32[728,8]{0,1:T(8,128)} %param.18) | copy-start | bytes 69892
  32.8 0.7 %copy-start.8 = (f32[8,128]{1,0:T(8,128)S(1)}, f32[8,128]{1,0:T(8,128)}, u32[]{:S(2)}) copy-start(f32[8,128]{1,0:T(8,128)} %get-tuple-element.7.coarse_ref) | copy-start | bytes 12292
  33.4 0.7 copy-start.9
  34.1 0.7 copy-start.10
  34.8 0.7 copy-start.11

commit v2 on v1

v2 whole, which is shorter than its diff:
```python
import functools
import math

import jax
import jax.numpy as jnp
import ml_dtypes
import numpy as np
from jax import lax
from jax.experimental import pallas as pl
from jax.experimental.pallas import tpu as pltpu
from jax.sharding import PartitionSpec as P

ORDER = 12
EQUIV_RADIUS = 2.95
CHECK_RADIUS = 1.05
SOFTEN_SQ = 0.0625
FOUR_PI = 4.0 * math.pi
MESH = pl.DeviceIdType.MESH

NPTS = 728
MAGS = 91
BLK = 96
WID = 8 * BLK
F32, BF16 = jnp.float32, jnp.bfloat16


def surface_points(edge_points):
    spacing = np.linspace(-1.0, 1.0, edge_points)
    lattice = np.stack(np.meshgrid(spacing, spacing, spacing, indexing="ij"), 0).reshape(3, -1)
    on_surface = np.max(np.abs(lattice), axis=0) > 0.999
    return lattice[:, on_surface].astype(np.float32)


def split2(value):
    hi = value.astype(ml_dtypes.bfloat16)
    lo = (value - hi.astype(np.float32)).astype(ml_dtypes.bfloat16)
    return hi, lo


@functools.lru_cache(maxsize=None)
def tables():
    points = surface_points(ORDER).astype(np.float64)
    grid = np.rint((points + 1.0) * (ORDER - 1) / 2.0).astype(int)
    index = {tuple(g): i for i, g in enumerate(grid.T)}
    half = ORDER // 2
    mags = [g for g in grid.T if min(g) >= half]
    order = np.full(WID, -1)
    for s in range(8):
        for m, g in enumerate(mags):
            key = tuple(g[a] if s >> a & 1 else ORDER - 1 - g[a] for a in range(3))
            order[BLK * s + m] = index[key]
    live = order >= 0
    placed = points[:, np.where(live, order, 0)]
    targets = -0.5 + 0.5 * CHECK_RADIUS * placed
    separation = targets[:, :, None] - EQUIV_RADIUS * placed[:, None, :]
    k0 = 1.0 / (FOUR_PI * np.sqrt(np.sum(separation * separation, 0)))
    k0 = np.where(live[:, None] & live[None, :], k0, 0.0).astype(np.float32)
    k_pair = np.concatenate(split2(k0), 1)
    perm = np.zeros((WID, WID), np.float32)
    perm[np.nonzero(live)[0], order[live]] = 1.0
    size = np.ones((3, BLK))
    size[:, :MAGS] = np.array([[points[a, index[tuple(g)]] for g in mags] for a in range(3)])
    rows = np.concatenate([2.0 * EQUIV_RADIUS * size, EQUIV_RADIUS**2 * np.sum(size * size, 0)[None]], 0)
    mag = np.broadcast_to(rows.astype(np.float32)[:, :, None], (4, BLK, 128)).copy()
    return k_pair, perm.astype(ml_dtypes.bfloat16), perm.T.copy().astype(ml_dtypes.bfloat16), mag


def pieces3(value):
    hi = value.astype(BF16).astype(F32)
    rest = value - hi
    mid = rest.astype(BF16).astype(F32)
    return hi, mid, (rest - mid).astype(BF16).astype(F32)


def mm(a, b):
    return jnp.dot(a, b, preferred_element_type=F32)


UNROLL = 4


def kernel(
    remote, *refs,
):
    if not remote:
        device_ref, coarse_in, win_in, *refs = refs
    (
        owner_ref, part_s, pan_s, count_s, tile_ref, counts_ref, coarse_hbm, panels_hbm, parts_hbm, pown_hbm, lown_hbm,
        m_hbm, k_hbm, perm_hbm, permt_hbm, mag_hbm, out_ref,
        coarse_ref, panels_ref, parts_ref, pown_ref, lown_ref, m_ref, k_ref, perm_ref, permt_ref, mag_ref, load_sem,
        line, picked, crossed, win, send1, recv1, send2, recv2, send3, recv3,
        m_pair, turn, pown, lown, hot, xrel, xf, xk, pf, pk, zb, slots, acc, uexp,
    ) = refs
    moves = {
        "coarse": (coarse_hbm, coarse_ref), "panels": (panels_hbm, panels_ref), "parts": (parts_hbm, parts_ref),
        "pown": (pown_hbm, pown_ref), "lown": (lown_hbm, lown_ref), "m": (m_hbm, m_ref.at[0:NPTS]),
        "k": (k_hbm, k_ref), "perm": (perm_hbm, perm_ref), "permt": (permt_hbm, permt_ref), "mag": (mag_hbm, mag_ref),
    }
    loads = {
        name: pltpu.make_async_copy(src, dst, load_sem.at[i]) for i, (name, (src, dst)) in enumerate(moves.items())
    }
    if remote:
        grp, box = lax.axis_index("grp"), lax.axis_index("box")
        row, col = box // 8, box % 8
        me = grp * 64 + box
        nxt, prv = lax.rem(me + 1, 512), lax.rem(me + 511, 512)
        cols = [row * 8 + lax.rem(col + r, 8) for r in range(1, 8)]
        rows = [lax.rem(row + r, 8) * 8 + col for r in range(1, 8)]
        beside = [(nxt // 64, nxt % 64), (prv // 64, prv % 64)]
        barrier = pltpu.get_barrier_semaphore()
        for other in cols + rows:
            pl.semaphore_signal(barrier, inc=1, device_id=(grp, other), device_id_type=MESH)
        for other in beside:
            pl.semaphore_signal(barrier, inc=1, device_id=other, device_id_type=MESH)
        device = me
    else:
        device = device_ref[0]
    for load in loads.values():
        load.start()

    first, halo, second = [], [], []
    loads["coarse"].wait()
    loads["panels"].wait()
    if remote:
        line[col] = jnp.zeros((8, 128), F32)
        for r in range(6):
            width = min(128, NPTS - 128 * r)
            line[col, r : r + 1, 0:width] = coarse_ref[0:1, 128 * r : 128 * r + width]
        win[1] = panels_ref[...]
        pl.semaphore_wait(barrier, 16)
        for r in range(1, 8):
            first.append(
                pltpu.make_async_remote_copy(
                    src_ref=line.at[col], dst_ref=line.at[col], send_sem=send1.at[r - 1], recv_sem=recv1.at[r - 1],
                    device_id=(grp, cols[r - 1]), device_id_type=MESH,
                )
            )
            first[-1].start()
        for r, other in enumerate(beside):
            halo.append(
                pltpu.make_async_remote_copy(
                    src_ref=win.at[1], dst_ref=win.at[2 * r], send_sem=send3.at[r], recv_sem=recv3.at[r],
                    device_id=other, device_id_type=MESH,
                )
            )
            halo[-1].start()
    else:
        for s in range(3):
            win[s] = win_in[s]

    lane = lax.broadcasted_iota(jnp.int32, (1, 128), 1)

    counts = counts_ref[...].astype(F32)
    g_row = lax.broadcasted_iota(jnp.int32, (64, 64), 0)
    g_col = lax.broadcasted_iota(jnp.int32, (64, 64), 1)
    upto = jnp.sum(jnp.where(g_col <= g_row, counts, 0.0), 1, keepdims=True)
    before = jnp.sum(jnp.where(g_col < g_row, counts, 0.0), 1, keepdims=True)
    leaf = lax.broadcasted_iota(jnp.int32, (64, 1), 0)
    local = []
    for a in range(3):
        c = jnp.bitwise_and(jnp.right_shift(leaf, a), 1) + 2 * jnp.bitwise_and(jnp.right_shift(leaf, 3 + a), 1)
        local.append((2 * c - 3).astype(F32))
    loads["parts"].wait()
    for n in range(16):
        index = (lax.broadcasted_iota(jnp.int32, (1, 128), 1) + 128 * n).astype(F32)
        inside = jnp.where((index >= before) & (index < upto), 1.0, 0.0)
        hot[n, 0:64] = inside.astype(BF16)
        hot[n, 64:128] = inside.astype(BF16)
        for a in range(3):
            centre = jnp.sum(inside * local[a], 0, keepdims=True)
            xrel[a : a + 1, 128 * n : 128 * n + 128] = parts_ref[a : a + 1, 128 * n : 128 * n + 128] + centre

    xf[...] = jnp.zeros_like(xf)
    x = xrel[0:3, :]
    hi, mid, low = pieces3(x)
    for r, piece in enumerate((hi, mid, hi, low, hi, mid)):
        xf[3 * r : 3 * r + 3, :] = piece
    for r, piece in enumerate(pieces3(jnp.sum(x * x, 0, keepdims=True))):
        xf[18 + r : 19 + r, :] = piece
    xf[21:24, :] = jnp.ones((3, 2048), F32)
    for n in range(16):
        xk[n] = xf[:, 128 * n : 128 * n + 128].astype(BF16)
    axis = lax.broadcasted_iota(jnp.int32, (4, 1), 0)
    shift = jnp.zeros((4, 1), jnp.int32)
    for b in range(3):
        bit = jnp.bitwise_and(jnp.right_shift(device, 3 * b + axis), 1)
        shift = shift + jnp.left_shift(bit, b)
    centre = jnp.where(axis < 3, (8 * shift + 4).astype(F32), 0.0)
    pf[28:128, :] = jnp.zeros((100, 1024), F32)

    def panel_part(s, keep):
        raw = win[s] * keep - centre
        z = raw[0:3]
        hi, mid, low = pieces3(z)
        for r, piece in enumerate((hi, hi, mid, hi, low, mid)):
            pf[3 * r : 3 * r + 3, :] = -2.0 * piece
        pf[18:21, :] = jnp.ones((3, 1024), F32)
        for r, piece in enumerate(pieces3(jnp.sum(z * z, 0, keepdims=True) + SOFTEN_SQ)):
            pf[21 + r : 22 + r, :] = piece
        pf[24:28, :] = raw

        for t in range(8):
            turned = pf[:, 128 * t : 128 * t + 128].T
            pk[8 * s + t] = turned[:, 0:32].astype(BF16)
            for a in range(4):
                zb[8 * s + t, a] = jnp.broadcast_to(turned[:, 24 + a : 25 + a], (128, 128))

    panel_part(1, 1.0)

    turn[:, 640:WID] = jnp.zeros((128, 128), F32)
    loads["pown"].wait()
    for k in range(8):
        value = jnp.broadcast_to(pown_ref[k : k + 1, :], (8, NPTS))
        turn[8 * k : 8 * k + 8, 0:NPTS] = value
        turn[64 + 8 * k : 72 + 8 * k, 0:NPTS] = value
    pown[...] = turn[...].T
    loads["lown"].wait()
    turn[0:64, 0:NPTS] = lown_ref[...]
    turn[64:128, 0:NPTS] = lown_ref[...]
    lown[...] = turn[...].T

    if remote:
        for copy in first:
            copy.wait()
        for r in range(8):
            there = lax.rem(row + r, 8) * 8 + col
            want = jnp.bitwise_and(owner_ref[grp * 64 + there], 7)
            if r == 0:
                crossed[row] = line[want]
            else:
                picked[r] = line[want]
        for r in range(1, 8):
            second.append(
                pltpu.make_async_remote_copy(
                    src_ref=picked.at[r], dst_ref=crossed.at[row], send_sem=send2.at[r - 1],
                    recv_sem=recv2.at[r - 1], device_id=(grp, rows[r - 1]), device_id_type=MESH,
                )
            )
            second[-1].start()

    m_pair[:, 640:WID] = jnp.zeros((WID, 128), BF16)
    m_pair[:, WID + 640 : 2 * WID] = jnp.zeros((WID, 128), BF16)
    m_ref[NPTS:WID] = jnp.zeros((WID - NPTS, NPTS), F32)
    loads["m"].wait()

    def m_split(r, carry):
        at = pl.ds(pl.multiple_of(r * 64, 64), 64)
        value = m_ref[at, :]
        hi = value.astype(BF16)
        m_pair[at, 0:NPTS] = hi
        m_pair[at, WID : WID + NPTS] = (value - hi.astype(F32)).astype(BF16)
        return carry

    lax.fori_loop(0, 12, m_split, 0)

    for copy in halo:
        copy.wait()
    panel_part(0, jnp.where(device == 0, 0.0, 1.0))
    panel_part(2, jnp.where(device == 511, 0.0, 1.0))

    def near_slots(i, carry):
        where = [i * UNROLL + u for u in range(UNROLL)]
        tiles = [pan_s[t] for t in where]
        squares = [mm(pk[tiles[u]], xk[part_s[where[u]]]) for u in range(UNROLL)]
        for u in range(UNROLL):
            sums = [jnp.zeros((8, 128), F32)] * 5
            z = [zb[tiles[u], a] for a in range(4)]
            for v in range(16):
                at = slice(8 * v, 8 * v + 8)
                inv = lax.rsqrt(squares[u][at])
                w = z[3][at] * inv
                w3 = w * (inv * inv)
                sums[0] = sums[0] + w
                sums[1] = sums[1] + w3
                for a in range(3):
                    sums[2 + a] = sums[2 + a] + w3 * z[a][at]
            at = pl.ds(pl.multiple_of(where[u] * 8, 8), 8)
            for q in range(5):
                slots[at, 128 * q : 128 * q + 128] = sums[q]
        return carry

    lax.fori_loop(0, 64 // UNROLL, near_slots, 0)
    slot = lax.broadcasted_iota(jnp.int32, (1, 64), 1)
    live = jnp.where(slot < count_s[0], tile_ref[...], 31).astype(F32)
    e_row = lax.broadcasted_iota(jnp.int32, (64, 512), 0)
    e_col = lax.broadcasted_iota(jnp.int32, (64, 512), 1)
    spread8 = jnp.where(jnp.right_shift(e_col, 3) == e_row, 1.0, 0.0).astype(BF16)
    target = mm(jnp.broadcast_to(live, (16, 64)).astype(BF16), spread8)
    n_row = lax.broadcasted_iota(jnp.int32, (16, 512), 0).astype(F32)
    choose = jnp.where(target == n_row, 1.0, 0.0).astype(BF16)
    hi, mid, low = pieces3(slots[...])
    acc[...] = mm(choose, hi.astype(BF16)) + (mm(choose, mid.astype(BF16)) + mm(choose, low.astype(BF16)))

    low_half = lane < 64
    column = jnp.bitwise_and(lane, 63)

    def swapped(value, octant):
        blocks = [value[BLK * s : BLK * s + BLK] for s in range(8)]
        for b in range(3):
            mask = jnp.bitwise_and(jnp.right_shift(octant, b), 1) == 1
            blocks = [jnp.where(mask, blocks[s ^ (1 << b)], blocks[s]) for s in range(8)]
        return jnp.concatenate(blocks, 0)

    def pieces(value):
        hi = value.astype(BF16).astype(F32)
        return jnp.where(low_half, hi, value - hi).astype(BF16)

    def both(pair_ref, x2):
        product = mm(pair_ref[:, 0:WID], x2) + mm(pair_ref[:, WID : 2 * WID], x2)
        return product + pltpu.roll(product, 64, 1)

    def level(x2, octant, own):
        placed = swapped(x2, octant).astype(BF16)
        checks = swapped(both(k_ref, placed), octant)
        back = mm(permt_ref[...], pieces(checks)).astype(BF16)
        return both(m_pair, back) + own

    loads["perm"].wait()
    loads["k"].wait()
    loads["permt"].wait()
    loads["mag"].wait()
    if remote:
        for copy in second:
            copy.wait()
        slot = jnp.bitwise_and(owner_ref[me], 63)
        coarse = crossed[jnp.right_shift(slot, 3)]
    else:
        coarse = coarse_in[...]
    half = lax.broadcasted_iota(jnp.int32, (128, 1), 0) < 64
    spread = []
    for r in range(6):
        value = coarse[r : r + 1, :]
        hi = value.astype(BF16).astype(F32)
        spread.append(jnp.where(half, hi, value - hi))
    spread = jnp.concatenate(spread, 1).astype(BF16)
    start = lax.dot_general(perm_ref[...], spread, (((1,), (1,)), ((), ())), preferred_element_type=F32)
    parents = level(start, jnp.right_shift(column, 3), pown[...])
    placed = mm(perm_ref[...], pieces(parents))
    leaves = level(placed, jnp.bitwise_and(column, 7), lown[...])
    dens = mm(perm_ref[...], pieces(leaves)).astype(BF16)

    def far_tile(n, carry):
        uexp[...] = mm(dens, hot[n])
        at = pl.ds(pl.multiple_of(n * 128, 128), 128)
        y = [jnp.broadcast_to(parts_ref[a : a + 1, at], (8, 128)) for a in range(3)]
        y2 = y[0] * y[0] + y[1] * y[1] + y[2] * y[2]
        pot = jnp.zeros((8, 128), F32)
        total = [jnp.zeros((8, 128), F32)] * 4
        for v in range(BLK // 8):
            band = slice(8 * v, 8 * v + 8)
            mags = [mag_ref[a, band] for a in range(3)]
            part = [y2 + mag_ref[3, band]]
            for a in range(3):
                step = y[a] * mags[a]
                part = [q + step for q in part] + [q - step for q in part]
            w3 = []
            for s in range(8):
                inv = lax.rsqrt(part[s])
                w = uexp[BLK * s + 8 * v : BLK * s + 8 * v + 8] * inv
                pot = pot + w
                w3.append(w * (inv * inv))
            x0 = [w3[s] + w3[s + 1] for s in (0, 2, 4, 6)]
            x1 = [w3[s + 1] - w3[s] for s in (0, 2, 4, 6)]
            y0 = [x0[s] + x0[s + 1] for s in (0, 2)]
            y1 = [x0[s + 1] - x0[s] for s in (0, 2)]
            total[0] = total[0] + (y0[0] + y0[1])
            total[1] = total[1] + ((x1[0] + x1[1]) + (x1[2] + x1[3])) * mags[0]
            total[2] = total[2] + (y1[0] + y1[1]) * mags[1]
            total[3] = total[3] + (y0[1] - y0[0]) * mags[2]
        mine = lax.broadcasted_iota(jnp.int32, (16, 128), 0) == n
        near = [
            jnp.sum(jnp.where(mine, acc[:, 128 * q : 128 * q + 128], 0.0), 0, keepdims=True) for q in range(5)
        ]
        scale = 1.0 / FOUR_PI
        out_ref[0:1, at] = scale * (jnp.sum(pot, 0, keepdims=True) + near[0])
        for a in range(3):
            whole = jnp.sum(y[a] * total[0] - 0.5 * total[1 + a], 0, keepdims=True)
            out_ref[1 + a : 2 + a, at] = -scale * (whole + (xrel[a : a + 1, at] * near[1] - near[2 + a]))
        return carry

    lax.fori_loop(0, 16, far_tile, 0)


def run(remote, *args):
    vmem = pl.BlockSpec(memory_space=pltpu.VMEM)
    smem = pl.BlockSpec(memory_space=pltpu.SMEM)
    anys = pl.BlockSpec(memory_space=pl.ANY)
    constants = [jnp.asarray(value) for value in tables()]
    dma = pltpu.SemaphoreType.DMA
    return pl.pallas_call(
        functools.partial(kernel, remote),
        out_shape=jax.ShapeDtypeStruct((4, 2048), F32),
        in_specs=([] if remote else [smem, vmem, vmem]) + [smem] * 4 + [vmem] * 2 + [anys] * 10,
        out_specs=vmem,
        scratch_shapes=[
            pltpu.VMEM((1, NPTS), F32),
            pltpu.VMEM((4, 1024), F32),
            pltpu.VMEM((3, 2048), F32),
            pltpu.VMEM((8, NPTS), F32),
            pltpu.VMEM((64, NPTS), F32),
            pltpu.VMEM((WID, NPTS), F32),
            pltpu.VMEM((WID, 2 * WID), BF16),
            pltpu.VMEM((WID, WID), BF16),
            pltpu.VMEM((WID, WID), BF16),
            pltpu.VMEM((4, BLK, 128), F32),
            dma((10,)),
            pltpu.VMEM((8, 8, 128), F32),
            pltpu.VMEM((8, 8, 128), F32),
            pltpu.VMEM((8, 8, 128), F32),
            pltpu.VMEM((3, 4, 1024), F32),
            dma((7,)),
            dma((7,)),
            dma((7,)),
            dma((7,)),
            dma((2,)),
            dma((2,)),
            pltpu.VMEM((WID, 2 * WID), BF16),
            pltpu.VMEM((128, WID), F32),
            pltpu.VMEM((WID, 128), F32),
            pltpu.VMEM((WID, 128), F32),
            pltpu.VMEM((16, 128, 128), BF16),
            pltpu.VMEM((8, 2048), F32),
            pltpu.VMEM((32, 2048), F32),
            pltpu.VMEM((16, 32, 128), BF16),
            pltpu.VMEM((128, 1024), F32),
            pltpu.VMEM((24, 128, 32), BF16),
            pltpu.VMEM((24, 4, 128, 128), F32),
            pltpu.VMEM((512, 640), F32),
            pltpu.VMEM((16, 640), F32),
            pltpu.VMEM((WID, 128), F32),
        ],
        compiler_params=pltpu.CompilerParams(
            vmem_limit_bytes=56 * 1024 * 1024, **(dict(collective_id=0, has_side_effects=True) if remote else {})
        ),
        name="downward",
    )(*args, *constants)


def per_device(
    coarse_dens, owner_slot, check_to_equiv, parent_own, leaf_own, leaf_counts, particles, panels, near_part,
    near_pan, near_count,
):
    return run(
        True, owner_slot, near_part, near_pan, near_count, near_part.reshape(1, 64), leaf_counts, coarse_dens.T, panels,
        particles, parent_own.T, leaf_own.T, check_to_equiv,
    )


def solution(mesh):
    both = ("grp", "box")
    placed = (
        P(None, both), P(), P(), P(None, both), P(None, both), P(both, None), P(None, both), P(None, both), P(both),
        P(both), P(both),
    )
    return jax.shard_map(per_device, mesh=mesh, in_specs=placed, out_specs=P(None, both), check_vma=False)
```

time: 67.3 us -> 44.5 us (0.66)
  the two profiles are of different devices: /device:TPU:2 before, /device:TPU:1 now
where the time goes in v2:
time: 44.5 us; the launch traced here: 44.3 us
  Pallas kernels  42.3 us (95%)
  local copies, waits for them, and re-layouts  1.38 us (3%)
  between operations  0.66 us (1%)
    pallas_call x1, Pallas kernels, run(): pl.pallas_call(functools.partial(kernel, remote), out_shape=jax.ShapeDtyp...  42.3 us
    unnamed x1, local copies, waits for them, and re-layouts  1.38 us

profile of v2, /device:TPU:1, one launch (start us, length us, event | category | flops | bytes accessed | tf_op | source)
XLA Modules:
  0.0 44.3 jit_solution(11516361860765438763)
XLA Ops:
  0.7 42.3 %downward.1 = f32[4,2048]{1,0:T(4,128)} custom-call(s32[512]{0:T(512)} %refs_0_.1, s32[64]{0:T(128)} %refs_1_.1, s32[64]{0:T(128)} %refs_2_.1, s32[1]{0:T(128)S(6)} %copy.17.refs_3_, s32[1,64]{1,0:T(1,128)} %bitcast.7, s32[1,64]{1,0:T(1,128)} %refs_5_.1, f32[1,728]{1,0:T(1,128)} %bitcast.6, f32[4,1024]{1,0:T(4,128)} %refs_7_.1, f32[3,2048]{1,0:T(4,128)} %refs_8_.1, ...), custom_call_target="tpu_custom_call" | custom-call | tf_op jit(solution)/shard_map/downward/pallas_call | solution.py:390
  42.9 1.4 %copy.18 = f32[4,2048]{1,0:T(4,128)} copy(f32[4,2048]{1,0:T(4,128)} %downward.1) | data formatting | bytes 65536

commit v3 on v2

v3 whole, which is shorter than its diff:
```python
import functools
import math

import jax
import jax.numpy as jnp
import ml_dtypes
import numpy as np
from jax import lax
from jax.experimental import pallas as pl
from jax.experimental.pallas import tpu as pltpu
from jax.sharding import PartitionSpec as P

ORDER = 12
EQUIV_RADIUS = 2.95
CHECK_RADIUS = 1.05
SOFTEN_SQ = 0.0625
FOUR_PI = 4.0 * math.pi
MESH = pl.DeviceIdType.MESH

NPTS = 728
MAGS = 91
BLK = 96
WID = 8 * BLK
F32, BF16 = jnp.float32, jnp.bfloat16


def surface_points(edge_points):
    spacing = np.linspace(-1.0, 1.0, edge_points)
    lattice = np.stack(np.meshgrid(spacing, spacing, spacing, indexing="ij"), 0).reshape(3, -1)
    on_surface = np.max(np.abs(lattice), axis=0) > 0.999
    return lattice[:, on_surface].astype(np.float32)


def split2(value):
    hi = value.astype(ml_dtypes.bfloat16)
    lo = (value - hi.astype(np.float32)).astype(ml_dtypes.bfloat16)
    return hi, lo


@functools.lru_cache(maxsize=None)
def tables():
    points = surface_points(ORDER).astype(np.float64)
    grid = np.rint((points + 1.0) * (ORDER - 1) / 2.0).astype(int)
    index = {tuple(g): i for i, g in enumerate(grid.T)}
    half = ORDER // 2
    mags = [g for g in grid.T if min(g) >= half]
    order = np.full(WID, -1)
    for s in range(8):
        for m, g in enumerate(mags):
            key = tuple(g[a] if s >> a & 1 else ORDER - 1 - g[a] for a in range(3))
            order[BLK * s + m] = index[key]
    live = order >= 0
    placed = points[:, np.where(live, order, 0)]
    targets = -0.5 + 0.5 * CHECK_RADIUS * placed
    separation = targets[:, :, None] - EQUIV_RADIUS * placed[:, None, :]
    k0 = 1.0 / (FOUR_PI * np.sqrt(np.sum(separation * separation, 0)))
    k0 = np.where(live[:, None] & live[None, :], k0, 0.0).astype(np.float32)
    k_pair = np.concatenate(split2(k0), 1)
    perm = np.zeros((WID, WID), np.float32)
    perm[np.nonzero(live)[0], order[live]] = 1.0
    size = np.ones((3, BLK))
    size[:, :MAGS] = np.array([[points[a, index[tuple(g)]] for g in mags] for a in range(3)])
    rows = np.concatenate([2.0 * EQUIV_RADIUS * size, EQUIV_RADIUS**2 * np.sum(size * size, 0)[None]], 0)
    mag = np.broadcast_to(rows.astype(np.float32)[:, :, None], (4, BLK, 128)).copy()
    return k_pair, perm.astype(ml_dtypes.bfloat16), perm.T.copy().astype(ml_dtypes.bfloat16), mag


def pieces3(value):
    hi = value.astype(BF16).astype(F32)
    rest = value - hi
    mid = rest.astype(BF16).astype(F32)
    return hi, mid, (rest - mid).astype(BF16).astype(F32)


def mm(a, b):
    return jnp.dot(a, b, preferred_element_type=F32)


UNROLL = 4


def kernel(
    remote, *refs,
):
    if not remote:
        device_ref, coarse_in, win_in, *refs = refs
    (
        owner_hbm, part_hbm, pan_hbm, count_hbm, tile_hbm, counts_hbm, coarse_hbm, panels_hbm, parts_hbm, pown_hbm, lown_hbm,
        m_hbm, k_hbm, perm_hbm, permt_hbm, mag_hbm, out_ref,
        owner_ref, part_s, pan_s, count_ref, tile_ref, counts_ref, coarse_ref, panels_ref, parts_ref, pown_ref, lown_ref, m_ref, k_ref, perm_ref, permt_ref, mag_ref, load_sem,
        line, picked, crossed, win, send1, recv1, send2, recv2, send3, recv3,
        m_half, m_pair, turn, pown, lown, hot, xrel, xf, xk, pf, pk, zb, slots, acc, uexp0, uexp1, sq0, sq1,
    ) = refs
    moves = {
        "coarse": (coarse_hbm, coarse_ref), "panels": (panels_hbm, panels_ref), "owner": (owner_hbm, owner_ref),
        "counts": (counts_hbm, counts_ref), "parts": (parts_hbm, parts_ref), "part": (part_hbm, part_s),
        "pan": (pan_hbm, pan_s), "count": (count_hbm, count_ref), "tile": (tile_hbm, tile_ref), "pown": (pown_hbm, pown_ref), "lown": (lown_hbm, lown_ref), "m": (m_hbm, m_ref.at[0:NPTS]),
        "permt": (permt_hbm, permt_ref), "perm": (perm_hbm, perm_ref), "k": (k_hbm, k_ref), "mag": (mag_hbm, mag_ref),
    }
    loads = {
        name: pltpu.make_async_copy(src, dst, load_sem.at[i]) for i, (name, (src, dst)) in enumerate(moves.items())
    }
    if remote:
        grp, box = lax.axis_index("grp"), lax.axis_index("box")
        row, col = box // 8, box % 8
        me = grp * 64 + box
        nxt, prv = lax.rem(me + 1, 512), lax.rem(me + 511, 512)
        cols = [row * 8 + lax.rem(col + r, 8) for r in range(1, 8)]
        rows = [lax.rem(row + r, 8) * 8 + col for r in range(1, 8)]
        beside = [(nxt // 64, nxt % 64), (prv // 64, prv % 64)]
        there = [me < 511, me > 0]
        greet = [jnp.logical_and(there[0], box != 63), there[1]]
        hear = [there[0], jnp.logical_and(there[1], box != 0)]
        answer = jnp.logical_and(there[1], box == 0)
        barrier = pltpu.get_barrier_semaphore()
        for other in rows + cols:
            pl.semaphore_signal(barrier, inc=1, device_id=(grp, other), device_id_type=MESH)
        for r in range(2):

            @pl.when(greet[r])
            def _(r=r):
                pl.semaphore_signal(barrier, inc=1, device_id=beside[r], device_id_type=MESH)

        device = me
    else:
        device = device_ref[0]
    for load in loads.values():
        load.start()
    if remote:
        first = [
            pltpu.make_async_remote_copy(
                src_ref=line.at[row], dst_ref=line.at[row], send_sem=send1.at[r], recv_sem=recv1.at[r],
                device_id=(grp, rows[r]), device_id_type=MESH,
            )
            for r in range(7)
        ]
        second = [
            pltpu.make_async_remote_copy(
                src_ref=picked.at[r], dst_ref=crossed.at[col], send_sem=send2.at[r], recv_sem=recv2.at[r],
                device_id=(grp, cols[r]), device_id_type=MESH,
            )
            for r in range(7)
        ]
        halo = [
            pltpu.make_async_remote_copy(
                src_ref=win.at[1], dst_ref=win.at[2 * r], send_sem=send3.at[r], recv_sem=recv3.at[r],
                device_id=beside[r], device_id_type=MESH,
            )
            for r in range(2)
        ]
    loads["coarse"].wait()
    loads["panels"].wait()
    loads["owner"].wait()
    if remote:
        line[row] = jnp.zeros((8, 128), F32)
        for r in range(6):
            width = min(128, NPTS - 128 * r)
            line[row, r : r + 1, 0:width] = coarse_ref[0:1, 128 * r : 128 * r + width]
        win[1] = panels_ref[...]
    else:
        for s in range(3):
            win[s] = win_in[s]

    lane = lax.broadcasted_iota(jnp.int32, (1, 128), 1)

    axis = lax.broadcasted_iota(jnp.int32, (4, 1), 0)
    shift = jnp.zeros((4, 1), jnp.int32)
    for b in range(3):
        bit = jnp.bitwise_and(jnp.right_shift(device, 3 * b + axis), 1)
        shift = shift + jnp.left_shift(bit, b)
    centre = jnp.where(axis < 3, (8 * shift + 4).astype(F32), 0.0)

    def panel_part(s):
        raw = win[s] - centre
        z = raw[0:3]
        hi, mid, low = pieces3(z)
        for r, piece in enumerate((hi, hi, mid, hi, low, mid)):
            pf[3 * r : 3 * r + 3, :] = -2.0 * piece
        pf[18:21, :] = jnp.ones((3, 1024), F32)
        for r, piece in enumerate(pieces3(jnp.sum(z * z, 0, keepdims=True) + SOFTEN_SQ)):
            pf[21 + r : 22 + r, :] = piece
        pf[24:28, :] = raw

        for t in range(8):
            turned = pf[:, 128 * t : 128 * t + 128].T
            operand = turned[:, 0:32].astype(BF16)
            pk[8 * s + t] = jnp.zeros((128, 128), BF16)
            pk[8 * s + t, :, 0:32] = operand
            pk[8 * s + t, :, 64:96] = operand
            for a in range(4):
                zb[8 * s + t, a] = jnp.broadcast_to(turned[:, 24 + a : 25 + a], (128, 128))

    def prepare():
        loads["counts"].wait()
        counts = counts_ref[...].astype(F32)
        g_row = lax.broadcasted_iota(jnp.int32, (64, 64), 0)
        g_col = lax.broadcasted_iota(jnp.int32, (64, 64), 1)
        upto = jnp.sum(jnp.where(g_col <= g_row, counts, 0.0), 1, keepdims=True)
        before = jnp.sum(jnp.where(g_col < g_row, counts, 0.0), 1, keepdims=True)
        leaf = lax.broadcasted_iota(jnp.int32, (64, 1), 0)
        local = []
        for a in range(3):
            c = jnp.bitwise_and(jnp.right_shift(leaf, a), 1) + 2 * jnp.bitwise_and(jnp.right_shift(leaf, 3 + a), 1)
            local.append((2 * c - 3).astype(F32))
        loads["parts"].wait()
        for n in range(16):
            index = (lax.broadcasted_iota(jnp.int32, (1, 128), 1) + 128 * n).astype(F32)
            inside = jnp.where((index >= before) & (index < upto), 1.0, 0.0)
            side = slice(128 * (n % 2), 128 * (n % 2) + 128)
            hot[n // 2, 0:64, side] = inside.astype(BF16)
            hot[n // 2, 64:128, side] = inside.astype(BF16)
            for a in range(3):
                centre = jnp.sum(inside * local[a], 0, keepdims=True)
                xrel[a : a + 1, 128 * n : 128 * n + 128] = parts_ref[a : a + 1, 128 * n : 128 * n + 128] + centre

        xf[...] = jnp.zeros_like(xf)
        x = xrel[0:3, :]
        hi, mid, low = pieces3(x)
        for r, piece in enumerate((hi, mid, hi, low, hi, mid)):
            xf[3 * r : 3 * r + 3, :] = piece
        for r, piece in enumerate(pieces3(jnp.sum(x * x, 0, keepdims=True))):
            xf[18 + r : 19 + r, :] = piece
        xf[21:24, :] = jnp.ones((3, 2048), F32)
        for n in range(16):
            xk[n] = xf[:, 128 * n : 128 * n + 128].astype(BF16)
        pf[28:128, :] = jnp.zeros((100, 1024), F32)
        panel_part(1)

        loads["perm"].wait()

        def placed_own():
            value = turn[...]
            hi = value.astype(BF16).astype(F32)
            both = jnp.where(lax.broadcasted_iota(jnp.int32, (128, 1), 0) < 64, hi, value - hi).astype(BF16)
            product = lax.dot_general(perm_ref[...], both, (((1,), (1,)), ((), ())), preferred_element_type=F32)
            return product + pltpu.roll(product, 64, 1)

        turn[:, 640:WID] = jnp.zeros((128, 128), F32)
        loads["pown"].wait()
        for k in range(8):
            value = jnp.broadcast_to(pown_ref[k : k + 1, :], (8, NPTS))
            turn[8 * k : 8 * k + 8, 0:NPTS] = value
            turn[64 + 8 * k : 72 + 8 * k, 0:NPTS] = value
        pown[...] = placed_own()
        loads["lown"].wait()
        turn[0:64, 0:NPTS] = lown_ref[...]
        turn[64:128, 0:NPTS] = lown_ref[...]
        lown[...] = placed_own()


    def prepare_m():
        m_ref[NPTS:WID] = jnp.zeros((WID - NPTS, NPTS), F32)
        loads["m"].wait()
        loads["permt"].wait()
        m_half[:, 640:WID] = jnp.zeros((WID, 128), BF16)
        m_half[:, WID + 640 : 2 * WID] = jnp.zeros((WID, 128), BF16)

        def m_split(r, carry):
            at = pl.ds(pl.multiple_of(r * 64, 64), 64)
            value = m_ref[at, :]
            hi = value.astype(BF16)
            m_half[at, 0:NPTS] = hi
            m_half[at, WID : WID + NPTS] = (value - hi.astype(F32)).astype(BF16)
            return carry

        lax.fori_loop(0, 12, m_split, 0)

        def m_columns(r, carry):
            at = pl.ds(pl.multiple_of(r * 256, 256), 256)
            for side in (slice(0, WID), slice(WID, 2 * WID)):
                m_half[at, side] = mm(m_half[at, side], permt_ref[...]).astype(BF16)
            return carry

        lax.fori_loop(0, 3, m_columns, 0)

        def m_rows(r, carry):
            at = pl.ds(pl.multiple_of(r * 256, 256), 256)
            m_pair[:, at] = mm(perm_ref[...], m_half[:, at]).astype(BF16)
            return carry

        lax.fori_loop(0, 6, m_rows, 0)


    if remote:
        early = box < 32

        @pl.when(early)
        def _():
            prepare()
            prepare_m()

        pl.semaphore_wait(barrier, 14 + hear[0].astype(jnp.int32) + hear[1].astype(jnp.int32))
        for copy in first:
            copy.start()
        for r in range(2):
            pl.when(hear[r])(halo[r].start)

        @pl.when(jnp.logical_not(early))
        def _():
            prepare()
            prepare_m()

        for copy in first:
            copy.wait()
        for r in range(8):
            whose = row * 8 + lax.rem(col + r, 8)
            want = jnp.bitwise_and(jnp.right_shift(owner_ref[grp * 64 + whose], 3), 7)
            if r == 0:
                crossed[col] = line[want]
            else:
                picked[r - 1] = line[want]
        for copy in second:
            copy.start()
        pl.when(there[1])(halo[0].wait_recv)
        pl.when(answer)(halo[1].start)
        pl.when(there[0])(halo[1].wait_recv)
        for r in range(2):
            pl.when(there[r])(halo[r].wait_send)

        @pl.when(jnp.logical_not(there[1]))
        def _():
            win[0] = jnp.zeros((4, 1024), F32)

        @pl.when(jnp.logical_not(there[0]))
        def _():
            win[2] = jnp.zeros((4, 1024), F32)

        panel_part(0)
        panel_part(2)
    else:
        prepare()
        prepare_m()
        panel_part(0)
        panel_part(2)

    loads["part"].wait()
    loads["pan"].wait()
    left = lax.broadcasted_iota(jnp.int32, (128, 128), 1) < 64
    blank = jnp.zeros((32, 128), BF16)

    def near_squares(i, into):
        for u in range(UNROLL // 2):
            t = i * UNROLL + 2 * u
            panel = jnp.where(left, pk[pan_s[t]], pk[pan_s[t + 1]])[:, 0:96]
            one, two = xk[part_s[t]], xk[part_s[t + 1]]
            part = jnp.concatenate(
                [jnp.concatenate([one, blank, blank], 0), jnp.concatenate([blank, blank, two], 0)], 1
            )
            into[u] = mm(panel, part)

    def near_sums(i, squares):
        for u in range(UNROLL):
            t = i * UNROLL + u
            tile = pan_s[t]
            side = slice(128 * (u % 2), 128 * (u % 2) + 128)
            sums = [jnp.zeros((8, 128), F32)] * 5
            for v in range(16):
                at = slice(8 * v, 8 * v + 8)
                inv = lax.rsqrt(squares[u // 2, at, side])
                w = zb[tile, 3, at] * inv
                w3 = w * (inv * inv)
                sums[0] = sums[0] + w
                sums[1] = sums[1] + w3
                for a in range(3):
                    sums[2 + a] = sums[2 + a] + w3 * zb[tile, a, at]
            at = pl.ds(pl.multiple_of(t * 8, 8), 8)
            for q in range(5):
                slots[at, 128 * q : 128 * q + 128] = sums[q]

    near_squares(0, sq0)
    steps = 64 // UNROLL

    def near_slots(i, carry):
        near_squares(2 * i + 1, sq1)
        near_sums(2 * i, sq0)
        near_squares(jnp.minimum(2 * i + 2, steps - 1), sq0)
        near_sums(2 * i + 1, sq1)
        return carry

    lax.fori_loop(0, steps // 2, near_slots, 0)
    loads["count"].wait()
    loads["tile"].wait()
    slot = lax.broadcasted_iota(jnp.int32, (1, 64), 1)
    live = jnp.where(slot < count_ref[0], tile_ref[...], 31).astype(F32)
    e_row = lax.broadcasted_iota(jnp.int32, (64, 512), 0)
    e_col = lax.broadcasted_iota(jnp.int32, (64, 512), 1)
    spread8 = jnp.where(jnp.right_shift(e_col, 3) == e_row, 1.0, 0.0).astype(BF16)
    target = mm(jnp.broadcast_to(live, (16, 64)).astype(BF16), spread8)
    n_row = lax.broadcasted_iota(jnp.int32, (16, 512), 0).astype(F32)
    choose = jnp.where(target == n_row, 1.0, 0.0).astype(BF16)
    hi, mid, low = pieces3(slots[...])
    acc[...] = mm(choose, hi.astype(BF16)) + (mm(choose, mid.astype(BF16)) + mm(choose, low.astype(BF16)))

    low_half = lane < 64
    column = jnp.bitwise_and(lane, 63)

    def swapped(value, octant):
        blocks = [value[BLK * s : BLK * s + BLK] for s in range(8)]
        for b in range(3):
            mask = jnp.bitwise_and(jnp.right_shift(octant, b), 1) == 1
            blocks = [jnp.where(mask, blocks[s ^ (1 << b)], blocks[s]) for s in range(8)]
        return jnp.concatenate(blocks, 0)

    def pieces(value):
        hi = value.astype(BF16).astype(F32)
        return jnp.where(low_half, hi, value - hi).astype(BF16)

    def both(pair_ref, x2):
        product = mm(pair_ref[...], jnp.concatenate([x2, x2], 0))
        return product + pltpu.roll(product, 64, 1)

    def level(x2, octant, own):
        checks = swapped(pieces(both(k_ref, swapped(x2, octant))), octant)
        return both(m_pair, checks) + own

    loads["k"].wait()
    loads["mag"].wait()
    if remote:
        for copy in second:
            copy.wait()
        slot = jnp.bitwise_and(owner_ref[me], 7)
        coarse = crossed[slot]
    else:
        coarse = coarse_in[...]
    half = lax.broadcasted_iota(jnp.int32, (128, 1), 0) < 64
    spread = []
    for r in range(6):
        value = coarse[r : r + 1, :]
        hi = value.astype(BF16).astype(F32)
        spread.append(jnp.where(half, hi, value - hi))
    spread = jnp.concatenate(spread, 1).astype(BF16)
    start = lax.dot_general(perm_ref[...], spread, (((1,), (1,)), ((), ())), preferred_element_type=F32)
    parents = level(start.astype(BF16), jnp.right_shift(column, 3), pown[...])
    leaves = level(pieces(parents), jnp.bitwise_and(column, 7), lown[...])
    dens = pieces(leaves)

    def far_tile(n, dense, side):
        at = pl.ds(pl.multiple_of(n * 128, 128), 128)
        y = [jnp.broadcast_to(parts_ref[a : a + 1, at], (8, 128)) for a in range(3)]
        y2 = y[0] * y[0] + y[1] * y[1] + y[2] * y[2]
        pot = jnp.zeros((8, 128), F32)
        total = [jnp.zeros((8, 128), F32)] * 4
        for v in range(BLK // 8):
            band = slice(8 * v, 8 * v + 8)
            mags = [mag_ref[a, band] for a in range(3)]
            part = [y2 + mag_ref[3, band]]
            for a in range(3):
                step = y[a] * mags[a]
                part = [q + step for q in part] + [q - step for q in part]
            w3 = []
            for s in range(8):
                inv = lax.rsqrt(part[s])
                w = dense[BLK * s + 8 * v : BLK * s + 8 * v + 8, side] * inv
                pot = pot + w
                w3.append(w * (inv * inv))
            x0 = [w3[s] + w3[s + 1] for s in (0, 2, 4, 6)]
            x1 = [w3[s + 1] - w3[s] for s in (0, 2, 4, 6)]
            y0 = [x0[s] + x0[s + 1] for s in (0, 2)]
            y1 = [x0[s + 1] - x0[s] for s in (0, 2)]
            total[0] = total[0] + (y0[0] + y0[1])
            total[1] = total[1] + ((x1[0] + x1[1]) + (x1[2] + x1[3])) * mags[0]
            total[2] = total[2] + (y1[0] + y1[1]) * mags[1]
            total[3] = total[3] + (y0[1] - y0[0]) * mags[2]
        mine = lax.broadcasted_iota(jnp.int32, (16, 128), 0) == n
        near = [
            jnp.sum(jnp.where(mine, acc[:, 128 * q : 128 * q + 128], 0.0), 0, keepdims=True) for q in range(5)
        ]
        scale = 1.0 / FOUR_PI
        out_ref[0:1, at] = scale * (jnp.sum(pot, 0, keepdims=True) + near[0])
        for a in range(3):
            whole = jnp.sum(y[a] * total[0] - 0.5 * total[1 + a], 0, keepdims=True)
            out_ref[1 + a : 2 + a, at] = -scale * (whole + (xrel[a : a + 1, at] * near[1] - near[2 + a]))

    uexp0[...] = mm(dens, hot[0])

    def far_pair(i, carry):
        uexp1[...] = mm(dens, hot[2 * i + 1])
        for h in range(2):
            far_tile(4 * i + h, uexp0, slice(128 * h, 128 * h + 128))
        uexp0[...] = mm(dens, hot[jnp.minimum(2 * i + 2, 7)])
        for h in range(2):
            far_tile(4 * i + 2 + h, uexp1, slice(128 * h, 128 * h + 128))
        return carry

    lax.fori_loop(0, 4, far_pair, 0)


def run(remote, *args):
    vmem = pl.BlockSpec(memory_space=pltpu.VMEM)
    smem = pl.BlockSpec(memory_space=pltpu.SMEM)
    anys = pl.BlockSpec(memory_space=pl.ANY)
    constants = [jnp.asarray(value) for value in tables()]
    dma = pltpu.SemaphoreType.DMA
    return pl.pallas_call(
        functools.partial(kernel, remote),
        out_shape=jax.ShapeDtypeStruct((4, 2048), F32),
        in_specs=([] if remote else [smem, vmem, vmem]) + [anys] * 16,
        out_specs=vmem,
        scratch_shapes=[
            pltpu.SMEM((512,), jnp.int32),
            pltpu.SMEM((64,), jnp.int32),
            pltpu.SMEM((64,), jnp.int32),
            pltpu.SMEM((1,), jnp.int32),
            pltpu.VMEM((1, 64), jnp.int32),
            pltpu.VMEM((1, 64), jnp.int32),
            pltpu.VMEM((1, NPTS), F32),
            pltpu.VMEM((4, 1024), F32),
            pltpu.VMEM((3, 2048), F32),
            pltpu.VMEM((8, NPTS), F32),
            pltpu.VMEM((64, NPTS), F32),
            pltpu.VMEM((WID, NPTS), F32),
            pltpu.VMEM((WID, 2 * WID), BF16),
            pltpu.VMEM((WID, WID), BF16),
            pltpu.VMEM((WID, WID), BF16),
            pltpu.VMEM((4, BLK, 128), F32),
            dma((16,)),
            pltpu.VMEM((8, 8, 128), F32),
            pltpu.VMEM((8, 8, 128), F32),
            pltpu.VMEM((8, 8, 128), F32),
            pltpu.VMEM((3, 4, 1024), F32),
            dma((7,)),
            dma((7,)),
            dma((7,)),
            dma((7,)),
            dma((2,)),
            dma((2,)),
            pltpu.VMEM((WID, 2 * WID), BF16),
            pltpu.VMEM((WID, 2 * WID), BF16),
            pltpu.VMEM((128, WID), F32),
            pltpu.VMEM((WID, 128), F32),
            pltpu.VMEM((WID, 128), F32),
            pltpu.VMEM((8, 128, 256), BF16),
            pltpu.VMEM((8, 2048), F32),
            pltpu.VMEM((32, 2048), F32),
            pltpu.VMEM((16, 32, 128), BF16),
            pltpu.VMEM((128, 1024), F32),
            pltpu.VMEM((24, 128, 128), BF16),
            pltpu.VMEM((24, 4, 128, 128), F32),
            pltpu.VMEM((512, 640), F32),
            pltpu.VMEM((16, 640), F32),
            pltpu.VMEM((WID, 256), F32),
            pltpu.VMEM((WID, 256), F32),
            pltpu.VMEM((UNROLL // 2, 128, 256), F32),
            pltpu.VMEM((UNROLL // 2, 128, 256), F32),
        ],
        compiler_params=pltpu.CompilerParams(
            vmem_limit_bytes=56 * 1024 * 1024, **(dict(collective_id=0, has_side_effects=True) if remote else {})
        ),
        name="downward",
    )(*args, *constants)


def per_device(
    coarse_dens, owner_slot, check_to_equiv, parent_own, leaf_own, leaf_counts, particles, panels, near_part,
    near_pan, near_count,
):
    return run(
        True, owner_slot, near_part, near_pan, near_count, near_part.reshape(1, 64), leaf_counts, coarse_dens.T, panels,
        particles, parent_own.T, leaf_own.T, check_to_equiv,
    )


def solution(mesh):
    both = ("grp", "box")
    placed = (
        P(None, both), P(), P(), P(None, both), P(None, both), P(both, None), P(None, both), P(None, both), P(both),
        P(both), P(both),
    )
    return jax.shard_map(per_device, mesh=mesh, in_specs=placed, out_specs=P(None, both), check_vma=False)
```

time: 44.5 us -> 40.3 us (0.906)
  Pallas kernels: 42.3 us -> 38 us
    pallas_call x1, Pallas kernels: 42.3 us -> 38 us  [run(): pl.pallas_call(functools.partial(kernel, remote), out_shape=jax.ShapeDtyp...]
where the time goes in v3:
time: 40.3 us; the launch traced here: 40.1 us
  Pallas kernels  38 us (94%)
  local copies, waits for them, and re-layouts  1.38 us (3%)
  between operations  0.66 us (2%)
    pallas_call x1, Pallas kernels, run(): pl.pallas_call(functools.partial(kernel, remote), out_shape=jax.ShapeDtyp...  38 us
    unnamed x1, local copies, waits for them, and re-layouts  1.38 us

profile of v3, /device:TPU:1, one launch (start us, length us, event | category | flops | bytes accessed | tf_op | source)
XLA Modules:
  0.0 40.1 jit_solution(8581886813356432786)
XLA Ops:
  0.7 38.0 %downward.1 = f32[4,2048]{1,0:T(4,128)} custom-call(s32[512]{0:T(512)} %refs_0_.1, s32[64]{0:T(128)} %refs_1_.1, s32[64]{0:T(128)} %refs_2_.1, s32[1]{0:T(128)S(6)} %copy.17.refs_3_, s32[1,64]{1,0:T(1,128)} %bitcast.7, s32[1,64]{1,0:T(1,128)} %refs_5_.1, f32[1,728]{1,0:T(1,128)} %bitcast.6, f32[4,1024]{1,0:T(4,128)} %refs_7_.1, f32[3,2048]{1,0:T(4,128)} %refs_8_.1, ...), custom_call_target="tpu_custom_call" | custom-call | tf_op jit(solution)/shard_map/downward/pallas_call | solution.py:494
  38.7 1.4 %copy.18 = f32[4,2048]{1,0:T(4,128)} copy(f32[4,2048]{1,0:T(4,128)} %downward.1) | data formatting | bytes 65536

commit v4 on v3

--- a/solution.py
+++ b/solution.py
@@ -76,7 +76,7 @@
     return jnp.dot(a, b, preferred_element_type=F32)
 
 
-UNROLL = 4
+UNROLL = 8
 
 
 def kernel(
@@ -85,51 +85,66 @@
     if not remote:
         device_ref, coarse_in, win_in, *refs = refs
     (
-        owner_hbm, part_hbm, pan_hbm, count_hbm, tile_hbm, counts_hbm, coarse_hbm, panels_hbm, parts_hbm, pown_hbm, lown_hbm,
+        owner_hbm, part_hbm, pan_hbm, count_ref, tile_hbm, counts_hbm, coarse_hbm, panels_hbm, parts_hbm, pown_hbm, lown_hbm,
         m_hbm, k_hbm, perm_hbm, permt_hbm, mag_hbm, out_ref,
-        owner_ref, part_s, pan_s, count_ref, tile_ref, counts_ref, coarse_ref, panels_ref, parts_ref, pown_ref, lown_ref, m_ref, k_ref, perm_ref, permt_ref, mag_ref, load_sem,
-        line, picked, crossed, win, send1, recv1, send2, recv2, send3, recv3,
+        owner_ref, part_s, pan_s, tile_ref, counts_ref, parts_ref, pown_ref, lown_ref, m_ref, k_ref, perm_ref, permt_ref, mag_ref, load_sem,
+        line, picked, crossed, win, relay, got, send1, recv1, send2, recv2, send3, recv3, send4, recv4,
         m_half, m_pair, turn, pown, lown, hot, xrel, xf, xk, pf, pk, zb, slots, acc, uexp0, uexp1, sq0, sq1,
     ) = refs
+    if remote:
+        grp, box = lax.axis_index("grp"), lax.axis_index("box")
+        row, col = box // 8, box % 8
+        me = grp * 64 + box
+        early = box < 32
+        late = box >= 32
+        nxt, prv = lax.rem(me + 1, 512), lax.rem(me + 511, 512)
+        cols = [row * 8 + lax.rem(col + r, 8) for r in range(1, 8)]
+        along, side = row % 4, row // 4
+        near_rows = [(side * 4 + lax.rem(along + r, 4)) * 8 + col for r in range(1, 4)]
+        far_rows = [((1 - side) * 4 + lax.rem(along + r, 4)) * 8 + col for r in range(4)]
+        rows = near_rows + far_rows
+        beside = [(nxt // 64, nxt % 64), (prv // 64, prv % 64)]
+        there = [me < 511, me > 0]
+        turned_back = jnp.logical_and(col == 0, box != 32)
+        greet = [
+            jnp.logical_and(there[0], jnp.logical_or(col != 7, box == 31)),
+            jnp.logical_and(there[1], box != 32),
+        ]
+        hear = [jnp.logical_and(there[0], box != 31), jnp.logical_and(there[1], jnp.logical_not(turned_back))]
+        answer = [box == 31, jnp.logical_and(there[1], turned_back)]
+        plain = jnp.logical_and(early, jnp.logical_and(box != 0, box != 31))
+        barrier = pltpu.get_barrier_semaphore()
+
+        @pl.when(early)
+        def _():
+            for other in near_rows + cols + far_rows:
+                pl.semaphore_signal(barrier, inc=1, device_id=(grp, other), device_id_type=MESH)
+
+        for r in range(2):
+
+            @pl.when(greet[r])
+            def _(r=r):
+                pl.semaphore_signal(barrier, inc=1, device_id=beside[r], device_id_type=MESH)
+
+        device = me
+    else:
+        row = 0
+        device = device_ref[0]
     moves = {
-        "coarse": (coarse_hbm, coarse_ref), "panels": (panels_hbm, panels_ref), "owner": (owner_hbm, owner_ref),
+        "coarse": (coarse_hbm, line.at[row]), "panels": (panels_hbm, win.at[1]), "owner": (owner_hbm, owner_ref),
         "counts": (counts_hbm, counts_ref), "parts": (parts_hbm, parts_ref), "part": (part_hbm, part_s),
-        "pan": (pan_hbm, pan_s), "count": (count_hbm, count_ref), "tile": (tile_hbm, tile_ref), "pown": (pown_hbm, pown_ref), "lown": (lown_hbm, lown_ref), "m": (m_hbm, m_ref.at[0:NPTS]),
+        "pan": (pan_hbm, pan_s), "tile": (tile_hbm, tile_ref), "pown": (pown_hbm, pown_ref), "lown": (lown_hbm, lown_ref), "m": (m_hbm, m_ref.at[0:NPTS]),
         "permt": (permt_hbm, permt_ref), "perm": (perm_hbm, perm_ref), "k": (k_hbm, k_ref), "mag": (mag_hbm, mag_ref),
     }
     loads = {
         name: pltpu.make_async_copy(src, dst, load_sem.at[i]) for i, (name, (src, dst)) in enumerate(moves.items())
     }
-    if remote:
-        grp, box = lax.axis_index("grp"), lax.axis_index("box")
-        row, col = box // 8, box % 8
-        me = grp * 64 + box
-        nxt, prv = lax.rem(me + 1, 512), lax.rem(me + 511, 512)
-        cols = [row * 8 + lax.rem(col + r, 8) for r in range(1, 8)]
-        rows = [lax.rem(row + r, 8) * 8 + col for r in range(1, 8)]
-        beside = [(nxt // 64, nxt % 64), (prv // 64, prv % 64)]
-        there = [me < 511, me > 0]
-        greet = [jnp.logical_and(there[0], box != 63), there[1]]
-        hear = [there[0], jnp.logical_and(there[1], box != 0)]
-        answer = jnp.logical_and(there[1], box == 0)
-        barrier = pltpu.get_barrier_semaphore()
-        for other in rows + cols:
-            pl.semaphore_signal(barrier, inc=1, device_id=(grp, other), device_id_type=MESH)
-        for r in range(2):
-
-            @pl.when(greet[r])
-            def _(r=r):
-                pl.semaphore_signal(barrier, inc=1, device_id=beside[r], device_id_type=MESH)
-
-        device = me
-    else:
-        device = device_ref[0]
     for load in loads.values():
         load.start()
     if remote:
         first = [
             pltpu.make_async_remote_copy(
-                src_ref=line.at[row], dst_ref=line.at[row], send_sem=send1.at[r], recv_sem=recv1.at[r],
+                src_ref=coarse_hbm, dst_ref=line.at[row], send_sem=send1.at[r], recv_sem=recv1.at[r],
                 device_id=(grp, rows[r]), device_id_type=MESH,
             )
             for r in range(7)
@@ -141,25 +156,17 @@
             )
             for r in range(7)
         ]
+        third = pltpu.make_async_remote_copy(
+            src_ref=relay, dst_ref=got, send_sem=send4.at[0], recv_sem=recv4.at[0],
+            device_id=(grp, far_rows[0]), device_id_type=MESH,
+        )
         halo = [
             pltpu.make_async_remote_copy(
-                src_ref=win.at[1], dst_ref=win.at[2 * r], send_sem=send3.at[r], recv_sem=recv3.at[r],
+                src_ref=panels_hbm, dst_ref=win.at[2 * r], send_sem=send3.at[r], recv_sem=recv3.at[r],
                 device_id=beside[r], device_id_type=MESH,
             )
             for r in range(2)
         ]
-    loads["coarse"].wait()
-    loads["panels"].wait()
-    loads["owner"].wait()
-    if remote:
-        line[row] = jnp.zeros((8, 128), F32)
-        for r in range(6):
-            width = min(128, NPTS - 128 * r)
-            line[row, r : r + 1, 0:width] = coarse_ref[0:1, 128 * r : 128 * r + width]
-        win[1] = panels_ref[...]
-    else:
-        for s in range(3):
-            win[s] = win_in[s]
 
     lane = lax.broadcasted_iota(jnp.int32, (1, 128), 1)
 
@@ -224,6 +231,7 @@
         for n in range(16):
             xk[n] = xf[:, 128 * n : 128 * n + 128].astype(BF16)
         pf[28:128, :] = jnp.zeros((100, 1024), F32)
+        loads["panels"].wait()
         panel_part(1)
 
         loads["perm"].wait()
@@ -281,57 +289,75 @@
         lax.fori_loop(0, 6, m_rows, 0)
 
 
+    def window():
+        if remote:
+            pl.when(there[1])(halo[0].wait_recv)
+            pl.when(answer[1])(halo[1].start)
+            pl.when(jnp.logical_and(there[0], jnp.logical_not(answer[0])))(halo[1].wait_recv)
+
+            @pl.when(jnp.logical_not(there[1]))
+            def _():
+                win[0] = jnp.zeros((4, 1024), F32)
+
+            @pl.when(jnp.logical_not(there[0]))
+            def _():
+                win[2] = jnp.zeros((4, 1024), F32)
+
+        panel_part(0)
+        panel_part(2)
+
     if remote:
-        early = box < 32
+        pl.when(early)(prepare)
+        heard = 4 + 6 * early.astype(jnp.int32) + hear[0].astype(jnp.int32) + hear[1].astype(jnp.int32)
+        pl.semaphore_wait(barrier, heard)
+
+        @pl.when(late)
+        def _():
+            for copy in first[3:]:
+                copy.start()
 
         @pl.when(early)
         def _():
-            prepare()
-            prepare_m()
-
-        pl.semaphore_wait(barrier, 14 + hear[0].astype(jnp.int32) + hear[1].astype(jnp.int32))
-        for copy in first:
-            copy.start()
+            for copy in first[:3]:
+                copy.start()
+
         for r in range(2):
             pl.when(hear[r])(halo[r].start)
-
-        @pl.when(jnp.logical_not(early))
-        def _():
-            prepare()
-            prepare_m()
-
-        for copy in first:
-            copy.wait()
-        for r in range(8):
-            whose = row * 8 + lax.rem(col + r, 8)
-            want = jnp.bitwise_and(jnp.right_shift(owner_ref[grp * 64 + whose], 3), 7)
-            if r == 0:
-                crossed[col] = line[want]
-            else:
-                picked[r - 1] = line[want]
-        for copy in second:
-            copy.start()
-        pl.when(there[1])(halo[0].wait_recv)
-        pl.when(answer)(halo[1].start)
-        pl.when(there[0])(halo[1].wait_recv)
-        for r in range(2):
-            pl.when(there[r])(halo[r].wait_send)
-
-        @pl.when(jnp.logical_not(there[1]))
-        def _():
-            win[0] = jnp.zeros((4, 1024), F32)
-
-        @pl.when(jnp.logical_not(there[0]))
-        def _():
-            win[2] = jnp.zeros((4, 1024), F32)
-
-        panel_part(0)
-        panel_part(2)
+        pl.when(late)(prepare)
+        prepare_m()
+        loads["owner"].wait()
+        loads["coarse"].wait()
+        pl.when(plain)(window)
+
+        @pl.when(answer[0])
+        def _():
+            halo[1].wait_recv()
+            halo[0].start()
+
+        @pl.when(early)
+        def _():
+            for copy in first:
+                copy.wait_recv()
+            for r in range(8):
+                for h in range(2):
+                    whose = (row + 4 * h) * 8 + lax.rem(col + r, 8)
+                    want = jnp.bitwise_and(jnp.right_shift(owner_ref[grp * 64 + whose], 3), 7)
+                    if r == 0:
+                        crossed[col, h] = line[want]
+                    else:
+                        picked[r - 1, h] = line[want]
+            for copy in second:
+                copy.start()
+
+        pl.when(jnp.logical_not(plain))(window)
     else:
         prepare()
+        win[0] = win_in[0]
+        win[2] = win_in[2]
+        loads["owner"].wait()
+        loads["coarse"].wait()
         prepare_m()
-        panel_part(0)
-        panel_part(2)
+        window()
 
     loads["part"].wait()
     loads["pan"].wait()
@@ -378,10 +404,9 @@
         return carry
 
     lax.fori_loop(0, steps // 2, near_slots, 0)
-    loads["count"].wait()
     loads["tile"].wait()
     slot = lax.broadcasted_iota(jnp.int32, (1, 64), 1)
-    live = jnp.where(slot < count_ref[0], tile_ref[...], 31).astype(F32)
+    live = jnp.where(slot < count_ref[...], tile_ref[...], 31).astype(F32)
     e_row = lax.broadcasted_iota(jnp.int32, (64, 512), 0)
     e_col = lax.broadcasted_iota(jnp.int32, (64, 512), 1)
     spread8 = jnp.where(jnp.right_shift(e_col, 3) == e_row, 1.0, 0.0).astype(BF16)
@@ -416,19 +441,23 @@
     loads["k"].wait()
     loads["mag"].wait()
     if remote:
-        for copy in second:
-            copy.wait()
-        slot = jnp.bitwise_and(owner_ref[me], 7)
-        coarse = crossed[slot]
+
+        @pl.when(early)
+        def _():
+            for copy in second:
+                copy.wait_recv()
+            got[...] = crossed[jnp.bitwise_and(owner_ref[me], 7), 0]
+            relay[...] = crossed[jnp.bitwise_and(owner_ref[me + 32], 7), 1]
+            third.start()
+
+        pl.when(late)(third.wait_recv)
+        coarse = got[...]
     else:
         coarse = coarse_in[...]
     half = lax.broadcasted_iota(jnp.int32, (128, 1), 0) < 64
-    spread = []
-    for r in range(6):
-        value = coarse[r : r + 1, :]
-        hi = value.astype(BF16).astype(F32)
-        spread.append(jnp.where(half, hi, value - hi))
-    spread = jnp.concatenate(spread, 1).astype(BF16)
+    hi = coarse.astype(BF16).astype(F32)
+    turn[:, 0:NPTS] = jnp.where(half, hi, coarse - hi)
+    spread = turn[...].astype(BF16)
     start = lax.dot_general(perm_ref[...], spread, (((1,), (1,)), ((), ())), preferred_element_type=F32)
     parents = level(start.astype(BF16), jnp.right_shift(column, 3), pown[...])
     leaves = level(pieces(parents), jnp.bitwise_and(column, 7), lown[...])
@@ -483,6 +512,19 @@
         return carry
 
     lax.fori_loop(0, 4, far_pair, 0)
+    if remote:
+        for r in range(2):
+            pl.when(there[r])(halo[r].wait_send)
+
+        @pl.when(early)
+        def _():
+            for copy in first[:3] + second + [third]:
+                copy.wait_send()
+
+        @pl.when(late)
+        def _():
+            for copy in first[3:]:
+                copy.wait_send()
 
 
 def run(remote, *args):
@@ -494,17 +536,14 @@
     return pl.pallas_call(
         functools.partial(kernel, remote),
         out_shape=jax.ShapeDtypeStruct((4, 2048), F32),
-        in_specs=([] if remote else [smem, vmem, vmem]) + [anys] * 16,
+        in_specs=([] if remote else [smem, vmem, vmem]) + [anys] * 3 + [vmem] + [anys] * 12,
         out_specs=vmem,
         scratch_shapes=[
             pltpu.SMEM((512,), jnp.int32),
             pltpu.SMEM((64,), jnp.int32),
             pltpu.SMEM((64,), jnp.int32),
-            pltpu.SMEM((1,), jnp.int32),
             pltpu.VMEM((1, 64), jnp.int32),
             pltpu.VMEM((1, 64), jnp.int32),
-            pltpu.VMEM((1, NPTS), F32),
-            pltpu.VMEM((4, 1024), F32),
             pltpu.VMEM((3, 2048), F32),
             pltpu.VMEM((8, NPTS), F32),
             pltpu.VMEM((64, NPTS), F32),
@@ -513,17 +552,21 @@
             pltpu.VMEM((WID, WID), BF16),
             pltpu.VMEM((WID, WID), BF16),
             pltpu.VMEM((4, BLK, 128), F32),
-            dma((16,)),
-            pltpu.VMEM((8, 8, 128), F32),
-            pltpu.VMEM((8, 8, 128), F32),
-            pltpu.VMEM((8, 8, 128), F32),
+            dma((15,)),
+            pltpu.VMEM((8, 1, NPTS), F32),
+            pltpu.VMEM((7, 2, 1, NPTS), F32),
+            pltpu.VMEM((8, 2, 1, NPTS), F32),
             pltpu.VMEM((3, 4, 1024), F32),
+            pltpu.VMEM((1, NPTS), F32),
+            pltpu.VMEM((1, NPTS), F32),
             dma((7,)),
             dma((7,)),
             dma((7,)),
             dma((7,)),
             dma((2,)),
             dma((2,)),
+            dma((1,)),
+            dma((1,)),
             pltpu.VMEM((WID, 2 * WID), BF16),
             pltpu.VMEM((WID, 2 * WID), BF16),
             pltpu.VMEM((128, WID), F32),
@@ -555,7 +598,7 @@
     near_pan, near_count,
 ):
     return run(
-        True, owner_slot, near_part, near_pan, near_count, near_part.reshape(1, 64), leaf_counts, coarse_dens.T, panels,
+        True, owner_slot, near_part, near_pan, near_count.reshape(1, 1), near_part.reshape(1, 64), leaf_counts, coarse_dens.T, panels,
         particles, parent_own.T, leaf_own.T, check_to_equiv,
     )
 

time: 40.3 us -> 37.9 us (0.940); the launches traced: 40.1 us -> 37.2 us
  Pallas kernels: 38 us -> 35.2 us
    pallas_call x1, Pallas kernels: 38 us -> 35.2 us  [run(): pl.pallas_call(functools.partial(kernel, remote), out_shape=jax.ShapeDtyp...]
where the time goes in v4:
time: 37.9 us; the launch traced here: 37.2 us
  Pallas kernels  35.2 us (93%)
  local copies, waits for them, and re-layouts  1.38 us (4%)
  between operations  0.66 us (2%)
    pallas_call x1, Pallas kernels, run(): pl.pallas_call(functools.partial(kernel, remote), out_shape=jax.ShapeDtyp...  35.2 us
    unnamed x1, local copies, waits for them, and re-layouts  1.38 us

profile of v4, /device:TPU:1, one launch (start us, length us, event | category | flops | bytes accessed | tf_op | source)
XLA Modules:
  0.0 37.2 jit_solution(7182658785480629843)
XLA Ops:
  0.7 35.2 %downward.1 = f32[4,2048]{1,0:T(4,128)} custom-call(s32[512]{0:T(512)} %refs_0_.1, s32[64]{0:T(128)} %refs_1_.1, s32[64]{0:T(128)} %refs_2_.1, s32[1,1]{1,0:T(1,128)} %bitcast.5.refs_3_, s32[1,64]{1,0:T(1,128)} %bitcast.9, s32[1,64]{1,0:T(1,128)} %refs_5_.1, f32[1,728]{1,0:T(1,128)} %bitcast.8, f32[4,1024]{1,0:T(4,128)} %refs_7_.1, f32[3,2048]{1,0:T(4,128)} %refs_8_.1, ...), custom_call_target="tpu_custom_call" | custom-call | tf_op jit(solution)/shard_map/downward/pallas_call | solution.py:536
  35.9 1.4 %copy.18 = f32[4,2048]{1,0:T(4,128)} copy(f32[4,2048]{1,0:T(4,128)} %downward.1) | data formatting | bytes 65536

commit v5 on v4

--- a/solution.py
+++ b/solution.py
@@ -88,8 +88,8 @@
         owner_hbm, part_hbm, pan_hbm, count_ref, tile_hbm, counts_hbm, coarse_hbm, panels_hbm, parts_hbm, pown_hbm, lown_hbm,
         m_hbm, k_hbm, perm_hbm, permt_hbm, mag_hbm, out_ref,
         owner_ref, part_s, pan_s, tile_ref, counts_ref, parts_ref, pown_ref, lown_ref, m_ref, k_ref, perm_ref, permt_ref, mag_ref, load_sem,
-        line, picked, crossed, win, relay, got, send1, recv1, send2, recv2, send3, recv3, send4, recv4,
-        m_half, m_pair, turn, pown, lown, hot, xrel, xf, xk, pf, pk, zb, slots, acc, uexp0, uexp1, sq0, sq1,
+        line, picked, crossed, win, relay, got, send1, recv1, send2, recv2, send3, recv3, send4, recv4, extra, send5, recv5,
+        m_half, m_pair, turn, pown, lown, hot, xrel, xf, xk, pf, pk, zb, slots, acc, uexp0, uexp1, sq0, sq1, inv_one, inv_cube,
     ) = refs
     if remote:
         grp, box = lax.axis_index("grp"), lax.axis_index("box")
@@ -105,20 +105,28 @@
         rows = near_rows + far_rows
         beside = [(nxt // 64, nxt % 64), (prv // 64, prv % 64)]
         there = [me < 511, me > 0]
-        turned_back = jnp.logical_and(col == 0, box != 32)
+        turned_back = jnp.logical_and(col == 0, jnp.logical_or(box == 0, box > 32))
         greet = [
-            jnp.logical_and(there[0], jnp.logical_or(col != 7, box == 31)),
+            jnp.logical_and(there[0], jnp.logical_or(col != 7, box <= 31)),
             jnp.logical_and(there[1], box != 32),
         ]
         hear = [jnp.logical_and(there[0], box != 31), jnp.logical_and(there[1], jnp.logical_not(turned_back))]
-        answer = [box == 31, jnp.logical_and(there[1], turned_back)]
-        plain = jnp.logical_and(early, jnp.logical_and(box != 0, box != 31))
+        answer = jnp.logical_and(there[1], turned_back)
+        plain = jnp.logical_and(early, jnp.logical_and(box != 0, col < 4))
         barrier = pltpu.get_barrier_semaphore()
 
         @pl.when(early)
         def _():
             for other in near_rows + cols + far_rows:
                 pl.semaphore_signal(barrier, inc=1, device_id=(grp, other), device_id_type=MESH)
+
+        @pl.when(box == 0)
+        def _():
+            pl.semaphore_signal(barrier, inc=1, device_id=(grp, 31), device_id_type=MESH)
+
+        @pl.when(box == 31)
+        def _():
+            pl.semaphore_signal(barrier, inc=1, device_id=(grp, 0), device_id_type=MESH)
 
         for r in range(2):
 
@@ -160,6 +168,14 @@
             src_ref=relay, dst_ref=got, send_sem=send4.at[0], recv_sem=recv4.at[0],
             device_id=(grp, far_rows[0]), device_id_type=MESH,
         )
+        lent = pltpu.make_async_remote_copy(
+            src_ref=panels_hbm, dst_ref=extra, send_sem=send5.at[0], recv_sem=recv5.at[0],
+            device_id=(grp, 0), device_id_type=MESH,
+        )
+        passed = pltpu.make_async_remote_copy(
+            src_ref=extra, dst_ref=win.at[0], send_sem=send5.at[1], recv_sem=recv5.at[1],
+            device_id=(grp, 32), device_id_type=MESH,
+        )
         halo = [
             pltpu.make_async_remote_copy(
                 src_ref=panels_hbm, dst_ref=win.at[2 * r], send_sem=send3.at[r], recv_sem=recv3.at[r],
@@ -289,11 +305,32 @@
         lax.fori_loop(0, 6, m_rows, 0)
 
 
+    def prepare_far():
+        loads["mag"].wait()
+
+        def distances(n, carry):
+            at = pl.ds(pl.multiple_of(n * 128, 128), 128)
+            y = [jnp.broadcast_to(parts_ref[a : a + 1, at], (8, 128)) for a in range(3)]
+            y2 = y[0] * y[0] + y[1] * y[1] + y[2] * y[2]
+            for v in range(BLK // 8):
+                band = slice(8 * v, 8 * v + 8)
+                part = [y2 + mag_ref[3, band]]
+                for a in range(3):
+                    step = y[a] * mag_ref[a, band]
+                    part = [q + step for q in part] + [q - step for q in part]
+                for s in range(8):
+                    inv = lax.rsqrt(part[s])
+                    inv_one[n, BLK * s + 8 * v : BLK * s + 8 * v + 8] = inv
+                    inv_cube[n, BLK * s + 8 * v : BLK * s + 8 * v + 8] = inv * (inv * inv)
+            return carry
+
+        lax.fori_loop(0, 16, distances, 0)
+
     def window():
         if remote:
-            pl.when(there[1])(halo[0].wait_recv)
-            pl.when(answer[1])(halo[1].start)
-            pl.when(jnp.logical_and(there[0], jnp.logical_not(answer[0])))(halo[1].wait_recv)
+            pl.when(jnp.logical_and(there[1], jnp.logical_not(jnp.logical_or(answer, box == 32))))(halo[0].wait_recv)
+            pl.when(there[0])(halo[1].wait_recv)
+            pl.when(box == 32)(passed.wait_recv)
 
             @pl.when(jnp.logical_not(there[1]))
             def _():
@@ -309,7 +346,9 @@
     if remote:
         pl.when(early)(prepare)
         heard = 4 + 6 * early.astype(jnp.int32) + hear[0].astype(jnp.int32) + hear[1].astype(jnp.int32)
+        heard = heard + jnp.logical_or(box == 0, box == 31).astype(jnp.int32)
         pl.semaphore_wait(barrier, heard)
+        pl.when(box == 31)(lent.start)
 
         @pl.when(late)
         def _():
@@ -325,19 +364,27 @@
             pl.when(hear[r])(halo[r].start)
         pl.when(late)(prepare)
         prepare_m()
+
+        @pl.when(jnp.logical_and(answer, late))
+        def _():
+            halo[0].wait_recv()
+            halo[1].start()
+
+        pl.when(jnp.logical_or(late, col < 4))(prepare_far)
         loads["owner"].wait()
         loads["coarse"].wait()
         pl.when(plain)(window)
 
-        @pl.when(answer[0])
-        def _():
-            halo[1].wait_recv()
-            halo[0].start()
-
         @pl.when(early)
         def _():
             for copy in first:
                 copy.wait_recv()
+
+            @pl.when(box == 0)
+            def _():
+                lent.wait_recv()
+                passed.start()
+
             for r in range(8):
                 for h in range(2):
                     whose = (row + 4 * h) * 8 + lax.rem(col + r, 8)
@@ -349,6 +396,11 @@
             for copy in second:
                 copy.start()
 
+        @pl.when(jnp.logical_and(answer, early))
+        def _():
+            halo[0].wait_recv()
+            halo[1].start()
+
         pl.when(jnp.logical_not(plain))(window)
     else:
         prepare()
@@ -357,6 +409,7 @@
         loads["owner"].wait()
         loads["coarse"].wait()
         prepare_m()
+        prepare_far()
         window()
 
     loads["part"].wait()
@@ -404,6 +457,8 @@
         return carry
 
     lax.fori_loop(0, steps // 2, near_slots, 0)
+    if remote:
+        pl.when(jnp.logical_and(early, col >= 4))(prepare_far)
     loads["tile"].wait()
     slot = lax.broadcasted_iota(jnp.int32, (1, 64), 1)
     live = jnp.where(slot < count_ref[...], tile_ref[...], 31).astype(F32)
@@ -439,7 +494,6 @@
         return both(m_pair, checks) + own
 
     loads["k"].wait()
-    loads["mag"].wait()
     if remote:
 
         @pl.when(early)
@@ -466,22 +520,17 @@
     def far_tile(n, dense, side):
         at = pl.ds(pl.multiple_of(n * 128, 128), 128)
         y = [jnp.broadcast_to(parts_ref[a : a + 1, at], (8, 128)) for a in range(3)]
-        y2 = y[0] * y[0] + y[1] * y[1] + y[2] * y[2]
         pot = jnp.zeros((8, 128), F32)
         total = [jnp.zeros((8, 128), F32)] * 4
         for v in range(BLK // 8):
             band = slice(8 * v, 8 * v + 8)
             mags = [mag_ref[a, band] for a in range(3)]
-            part = [y2 + mag_ref[3, band]]
-            for a in range(3):
-                step = y[a] * mags[a]
-                part = [q + step for q in part] + [q - step for q in part]
             w3 = []
             for s in range(8):
-                inv = lax.rsqrt(part[s])
-                w = dense[BLK * s + 8 * v : BLK * s + 8 * v + 8, side] * inv
-                pot = pot + w
-                w3.append(w * (inv * inv))
+                at8 = slice(BLK * s + 8 * v, BLK * s + 8 * v + 8)
+                u = dense[at8, side]
+                pot = pot + u * inv_one[n, at8]
+                w3.append(u * inv_cube[n, at8])
             x0 = [w3[s] + w3[s + 1] for s in (0, 2, 4, 6)]
             x1 = [w3[s + 1] - w3[s] for s in (0, 2, 4, 6)]
             y0 = [x0[s] + x0[s + 1] for s in (0, 2)]
@@ -513,8 +562,10 @@
 
     lax.fori_loop(0, 4, far_pair, 0)
     if remote:
-        for r in range(2):
-            pl.when(there[r])(halo[r].wait_send)
+        pl.when(jnp.logical_and(there[0], box != 31))(halo[0].wait_send)
+        pl.when(there[1])(halo[1].wait_send)
+        pl.when(box == 31)(lent.wait_send)
+        pl.when(box == 0)(passed.wait_send)
 
         @pl.when(early)
         def _():
@@ -567,6 +618,9 @@
             dma((2,)),
             dma((1,)),
             dma((1,)),
+            pltpu.VMEM((4, 1024), F32),
+            dma((2,)),
+            dma((2,)),
             pltpu.VMEM((WID, 2 * WID), BF16),
             pltpu.VMEM((WID, 2 * WID), BF16),
             pltpu.VMEM((128, WID), F32),
@@ -585,6 +639,8 @@
             pltpu.VMEM((WID, 256), F32),
             pltpu.VMEM((UNROLL // 2, 128, 256), F32),
             pltpu.VMEM((UNROLL // 2, 128, 256), F32),
+            pltpu.VMEM((16, WID, 128), F32),
+            pltpu.VMEM((16, WID, 128), F32),
         ],
         compiler_params=pltpu.CompilerParams(
             vmem_limit_bytes=56 * 1024 * 1024, **(dict(collective_id=0, has_side_effects=True) if remote else {})

time: 37.9 us -> 37.7 us (level); the launches traced: 37.2 us -> 37.5 us
  no operation moved by 1% of the time
where the time goes in v5:
time: 37.7 us; the launch traced here: 37.5 us
  Pallas kernels  35.4 us (94%)
  local copies, waits for them, and re-layouts  1.38 us (4%)
  between operations  0.66 us (2%)
    pallas_call x1, Pallas kernels, run(): pl.pallas_call(functools.partial(kernel, remote), out_shape=jax.ShapeDtyp...  35.4 us
    unnamed x1, local copies, waits for them, and re-layouts  1.38 us

profile of v5, /device:TPU:1, one launch (start us, length us, event | category | flops | bytes accessed | tf_op | source)
XLA Modules:
  0.0 37.5 jit_solution(12099749054348370505)
XLA Ops:
  0.7 35.4 %downward.1 = f32[4,2048]{1,0:T(4,128)} custom-call(s32[512]{0:T(512)} %refs_0_.1, s32[64]{0:T(128)} %refs_1_.1, s32[64]{0:T(128)} %refs_2_.1, s32[1,1]{1,0:T(1,128)} %bitcast.5.refs_3_, s32[1,64]{1,0:T(1,128)} %bitcast.9, s32[1,64]{1,0:T(1,128)} %refs_5_.1, f32[1,728]{1,0:T(1,128)} %bitcast.8, f32[4,1024]{1,0:T(4,128)} %refs_7_.1, f32[3,2048]{1,0:T(4,128)} %refs_8_.1, ...), custom_call_target="tpu_custom_call" | custom-call | tf_op jit(solution)/shard_map/downward/pallas_call | solution.py:587
  36.1 1.4 %copy.18 = f32[4,2048]{1,0:T(4,128)} copy(f32[4,2048]{1,0:T(4,128)} %downward.1) | data formatting | bytes 65536

commit v6 on v5

--- a/solution.py
+++ b/solution.py
@@ -326,22 +326,30 @@
 
         lax.fori_loop(0, 16, distances, 0)
 
-    def window():
+    def window_next():
         if remote:
+            pl.when(there[0])(halo[1].wait_recv)
+
+            @pl.when(jnp.logical_not(there[0]))
+            def _():
+                win[2] = jnp.zeros((4, 1024), F32)
+
+        panel_part(2)
+
+    def window_previous():
+        if remote:
+            pl.when(box == 32)(passed.wait_recv)
             pl.when(jnp.logical_and(there[1], jnp.logical_not(jnp.logical_or(answer, box == 32))))(halo[0].wait_recv)
-            pl.when(there[0])(halo[1].wait_recv)
-            pl.when(box == 32)(passed.wait_recv)
 
             @pl.when(jnp.logical_not(there[1]))
             def _():
                 win[0] = jnp.zeros((4, 1024), F32)
 
-            @pl.when(jnp.logical_not(there[0]))
-            def _():
-                win[2] = jnp.zeros((4, 1024), F32)
-
         panel_part(0)
-        panel_part(2)
+
+    def window():
+        window_next()
+        window_previous()
 
     if remote:
         pl.when(early)(prepare)
@@ -396,12 +404,14 @@
             for copy in second:
                 copy.start()
 
+        pl.when(jnp.logical_not(plain))(window_next)
+
         @pl.when(jnp.logical_and(answer, early))
         def _():
             halo[0].wait_recv()
             halo[1].start()
 
-        pl.when(jnp.logical_not(plain))(window)
+        pl.when(jnp.logical_not(plain))(window_previous)
     else:
         prepare()
         win[0] = win_in[0]

time: 37.7 us -> 36.7 us (0.973)
  Pallas kernels: 35.4 us -> 34.5 us
    pallas_call x1, Pallas kernels: 35.4 us -> 34.5 us  [run(): pl.pallas_call(functools.partial(kernel, remote), out_shape=jax.ShapeDtyp...]
where the time goes in v6:
time: 36.7 us; the launch traced here: 36.6 us
  Pallas kernels  34.5 us (94%)
  local copies, waits for them, and re-layouts  1.38 us (4%)
  between operations  0.66 us (2%)
    pallas_call x1, Pallas kernels, run(): pl.pallas_call(functools.partial(kernel, remote), out_shape=jax.ShapeDtyp...  34.5 us
    unnamed x1, local copies, waits for them, and re-layouts  1.38 us

profile of v6, /device:TPU:1, one launch (start us, length us, event | category | flops | bytes accessed | tf_op | source)
XLA Modules:
  0.0 36.6 jit_solution(1200624857933709452)
XLA Ops:
  0.7 34.5 %downward.1 = f32[4,2048]{1,0:T(4,128)} custom-call(s32[512]{0:T(512)} %refs_0_.1, s32[64]{0:T(128)} %refs_1_.1, s32[64]{0:T(128)} %refs_2_.1, s32[1,1]{1,0:T(1,128)} %bitcast.5.refs_3_, s32[1,64]{1,0:T(1,128)} %bitcast.9, s32[1,64]{1,0:T(1,128)} %refs_5_.1, f32[1,728]{1,0:T(1,128)} %bitcast.8, f32[4,1024]{1,0:T(4,128)} %refs_7_.1, f32[3,2048]{1,0:T(4,128)} %refs_8_.1, ...), custom_call_target="tpu_custom_call" | custom-call | tf_op jit(solution)/shard_map/downward/pallas_call | solution.py:597
  35.2 1.4 %copy.18 = f32[4,2048]{1,0:T(4,128)} copy(f32[4,2048]{1,0:T(4,128)} %downward.1) | data formatting | bytes 65536
